TPU v7x, 128 devices: a whole 4x4x4 slice. The times are simulated.
128 devices in a mesh: row: 8 (over y, core), col: 16 (over x, z).
Axes of the slice: x: 4, y: 4, z: 4, core: 2. Of those that a mesh axis runs over, the one named last changes fastest.
Arguments:
- tokens: bfloat16 [1024, 18432], P(None, ('row', 'col')), may hold values from -200 to 200
- layer_norm_gain: bfloat16 [18432], P(('row', 'col')), may hold values from 0.099609375 to 1.8984375
- query_weight: bfloat16 [18432, 12288], P('row', 'col'), may hold values from -0.046875 to 0.046875
- kv_weight: bfloat16 [18432, 512], P('row'), may hold values from -0.046875 to 0.046875
- output_weight_matrix: bfloat16 [12288, 18432], P('col', 'row'), may hold values from -0.5 to 0.5
- kv_cache: bfloat16 [1024, 2048, 512], P(('row', 'col')), may hold values from -1000 to 1000
- lengths: int32 [1024], P(('row', 'col')), may hold values from 2 to 2048, as said below
Outputs:
- branch: bfloat16 [1024, 18432], P(None, ('row', 'col'))
- new_kv: bfloat16 [1024, 512], P(('row', 'col'))
Inputs may be any that keep to these rules, and one draw needn't show every extreme that they name: `lengths`: some row has exactly 2048 valid positions and some row exactly 2.
All inputs are finite; a program needn't handle non-finite values.
Results may differ from a plain program's by a relative error of at most 0.02.
Values may be sent and summed in bfloat16 or wider, within the bound.
A program may use at most 128 MiB of HBM per device.

v0:
```python
import jax
import jax.numpy as jnp
from jax import lax
from jax.sharding import PartitionSpec as P

D = 18432
HEADS = 48
HD = 256


EPSILON = 1e-05
NEGATIVE_FLOOR = -1e30


def normalize(value_rows, gain, total_sum, total_sq, width):
    floats = value_rows.astype(jnp.float32)
    average = total_sum / width
    inverse = lax.rsqrt(total_sq / width - average * average + EPSILON)
    return (floats - average[:, None]) * inverse[:, None] * gain.astype(jnp.float32)[None, :]


def own_rows(matrix, row_count, col_count, col_index):
    shaped = matrix.reshape(row_count, col_count, -1, matrix.shape[-1])
    picked = lax.dynamic_index_in_dim(shaped, col_index, 1, keepdims=False)
    return picked.reshape(-1, matrix.shape[-1])


def attend(queries, cache, fresh, lengths, count, block_len):
    head_dim = queries.shape[2]
    score_scale = head_dim ** (-0.5)
    new_keys = fresh[:, :head_dim]
    new_values = fresh[:, head_dim:]
    new_scores = (
        jnp.einsum("bhd,bd->bh", queries, new_keys, preferred_element_type=jnp.float32)
        * score_scale
    )

    def block_scores(step_index):
        kv_block = lax.dynamic_slice_in_dim(cache, step_index * block_len, block_len, 1)
        scores = (
            jnp.einsum(
                "mqg,mfg->mqf",
                queries,
                kv_block[:, :, :head_dim],
                preferred_element_type=jnp.float32,
            )
            * score_scale
        )
        position = step_index * block_len + jnp.arange(block_len, dtype=jnp.int32)
        valid = (position[None, :] < lengths[:, None])[:, None, :]
        return (jnp.where(valid, scores, NEGATIVE_FLOOR), valid, kv_block[:, :, head_dim:])

    def find_max(step_index, running):
        scores, valid, value_rows = block_scores(step_index)
        return jnp.maximum(running, jnp.max(scores, axis=2))

    highest = lax.fori_loop(0, count, find_max, new_scores)

    def accumulate(step_index, carry):
        weight_sum, context = carry
        scores, valid, value_rows = block_scores(step_index)
        attention_probabilities = jnp.where(valid, jnp.exp(scores - highest[:, :, None]), 0.0)
        weight_sum = weight_sum + jnp.sum(attention_probabilities, axis=2)
        context = context + jnp.einsum(
            "ruf,rfs->rus",
            attention_probabilities.astype(jnp.bfloat16),
            value_rows,
            preferred_element_type=jnp.float32,
        )
        return (weight_sum, context)

    new_probs = jnp.exp(new_scores - highest)
    first_context = (
        new_probs.astype(jnp.bfloat16).astype(jnp.float32)[:, :, None]
        * new_values.astype(jnp.float32)[:, None, :]
    )
    weight_sum, context = lax.fori_loop(0, count, accumulate, (new_probs, first_context))
    return (context / weight_sum[:, :, None]).astype(jnp.bfloat16)


def shards(
    tokens, layer_norm_gain, query_weight, kv_weight, output_weight_matrix, kv_cache, lengths
):
    row_count = lax.axis_size("row")
    col_count = lax.axis_size("col")
    col_index = lax.axis_index("col")
    rows_dev = kv_cache.shape[0]
    head_cols = query_weight.shape[1]
    kv_cols = kv_weight.shape[1]
    floats = tokens.astype(jnp.float32)
    total_sum, total_sq = lax.psum(
        (jnp.sum(floats, axis=1), jnp.sum(floats * floats, axis=1)), ("row", "col")
    )
    normed = normalize(tokens, layer_norm_gain, total_sum, total_sq, D).astype(jnp.bfloat16)
    portion = lax.all_gather(normed, "col", axis=1, tiled=True)
    query_acc = jnp.dot(portion, query_weight, preferred_element_type=jnp.float32)
    selected = own_rows(portion, row_count, col_count, col_index)
    kv_acc = jnp.dot(selected, kv_weight, preferred_element_type=jnp.float32)
    query_four = query_acc.reshape(row_count, col_count, rows_dev, head_cols)
    kv_three = kv_acc.reshape(row_count, rows_dev, kv_cols)
    moved = lax.all_to_all(query_four, "col", split_axis=1, concat_axis=3, tiled=True)
    query_sum, kv_sum = (
        lax.psum_scatter(moved, "row", scatter_dimension=0, tiled=True),
        lax.psum_scatter(kv_three, "row", scatter_dimension=0, tiled=True),
    )
    queries = query_sum[0, 0].astype(jnp.bfloat16)
    new_kv = kv_sum[0].astype(jnp.bfloat16)
    queries = queries.reshape(rows_dev, HEADS, HD)
    block_len = min(512, kv_cache.shape[1])
    count = kv_cache.shape[1] // block_len
    context = attend(queries, kv_cache, new_kv, lengths, count, block_len)
    context = context.reshape(1, rows_dev, HEADS * HD)
    returned = lax.all_to_all(context, "col", split_axis=2, concat_axis=0, tiled=True)
    returned = returned.reshape(col_count * rows_dev, head_cols)
    out_term = jnp.dot(
        lax.all_gather(returned, "row", axis=0, tiled=True),
        output_weight_matrix,
        preferred_element_type=jnp.float32,
    )
    branch = lax.psum_scatter(out_term.astype(jnp.bfloat16), "col", scatter_dimension=1, tiled=True)
    return (branch, new_kv)


def solution(mesh):
    placed = (
        P(None, ("row", "col")),
        P(("row", "col")),
        P("row", "col"),
        P("row", None),
        P("col", "row"),
        P(("row", "col"), None, None),
        P(("row", "col")),
    )
    return jax.shard_map(
        shards,
        mesh=mesh,
        in_specs=placed,
        out_specs=(P(None, ("row", "col")), P(("row", "col"), None)),
        check_vma=False,
    )
```

profile of v0, /device:TPU:8, one launch (start us, length us, event | category | flops | bytes accessed | tf_op | source)
XLA Modules:
  0.0 511.7 jit_solution(12558281289858238281)
XLA Ops:
  7.2 1.2 convert_reduce_fusion
  8.4 1.2 convert_element_type.46
  9.7 66.7 %all-reduce = (f32[1024]{0:T(1024)S(1)}, f32[1024]{0:T(1024)S(1)}) all-reduce(f32[1024]{0:T(1024)S(1)} %get-tuple-element.237, f32[1024]{0:T(1024)S(1)} %get-tuple-element.236), channel_id=1, replica_groups=mesh['row'=8,'col'=16] {'row','col'}, use_global_device_ids=true, to_apply=%region_3.0 | all-reduce | flops 2048 | bytes 16384 | tf_op jit(solution)/shard_map/psum | solution.py:91
  76.3 1.8 fusion.44
  78.2 51.8 %all-gather.3.cloned.1.call-done = bf16[1024,2304]{0,1:T(8,128)(2,1)} async-done(((bf16[1024,144]{0,1:T(8,128)(2,1)}), bf16[1024,2304]{0,1:T(8,128)(2,1)}) %all-gather.3.cloned.1.call-update) | async-done | bytes 4718608 | tf_op jit(solution)/shard_map/all_gather | solution.py:95
  130.0 6.9 %fusion.53 = f32[1024,768]{1,0:T(8,128)S(1)} fusion(bf16[1024,2304]{0,1:T(8,128)(2,1)} %all-gather.3.cloned.1.call-done, bf16[2304,768]{1,0:T(8,128)(2,1)} %param.13), kind=kOutput, calls=%fused_computation.53 | convolution fusion | flops 3623878656 | bytes 11403264 | tf_op jit(solution)/shard_map/dot_general | solution.py:96
  136.8 2.0 copy.14
  138.8 5.3 %all-to-all-start = ((f32[8,16,8,768]{3,2,0,1:T(8,128)}), f32[8,16,8,768]{3,2,0,1:T(8,128)}, u32[]{:S(2)}, u32[]{:S(2)}) async-start(f32[8,16,8,768]{3,2,0,1:T(8,128)} %copy.14), calls=%async_computation | async-start | bytes 6291456 | tf_op jit(solution)/shard_map/all_to_all | solution.py:101
  144.2 6.8 %copy.16 = bf16[1024,2304]{1,0:T(8,128)(2,1)} copy(bf16[1024,2304]{0,1:T(8,128)(2,1)} %all-gather.3.cloned.1.call-done) | data formatting | bytes 9437184 | tf_op jit(solution)/shard_map/all_gather | solution.py:95
  151.0 3.0 fusion.40
  154.0 32.6 %all-to-all-done = f32[8,16,8,768]{3,2,0,1:T(8,128)} async-done(((f32[8,16,8,768]{3,2,0,1:T(8,128)}), f32[8,16,8,768]{3,2,0,1:T(8,128)}, u32[]{:S(2)}, u32[]{:S(2)}) %all-to-all-start) | async-done | bytes 3145760 | tf_op jit(solution)/shard_map/all_to_all | solution.py:101
  186.6 3.8 copy.24
  190.8 0.7 convert_bitcast_fusion
  191.5 0.6 copy-done.2
  192.1 0.6 slice_convert_fusion
  192.7 32.5 %reduce-scatter.4.cloned.1.call-done = f32[1,1,8,12288]{3,2,0,1:T(8,128)} async-done(((f32[8,1,8,12288]{3,2,0,1:T(8,128)}), f32[1,1,8,12288]{3,2,0,1:T(8,128)}) %reduce-scatter.4.cloned.1.call-update) | async-done | bytes 393232 | tf_op jit(solution)/shard_map/reduce_scatter | solution.py:103
  225.1 1.0 convert_element_type.48
  226.2 0.7 copy.17
  227.0 0.6 copy-done.3
  227.6 10.1 %while.28 = (s32[]{:T(128)}, f32[8,48]{1,0:T(8,128)S(1)}, s32[8]{0:T(128)S(1)}, bf16[8,2048,512]{2,1,0:T(8,128)(2,1)}, bf16[8,48,256]{2,1,0:T(8,128)(2,1)}, /*index=5*/s32[]{:T(128)}, s32[]{:T(128)}, s32[]{:T(128)}, s32[]{:T(128)}) while((s32[]{:T(128)}, f32[8,48]{1,0:T(8,128)S(1)}, s32[8]{0:T(128)S(1)}, bf16[8,2048,512]{2,1,0:T(8,128)(2,1)}, ...), condition=%wide.region_8.9_spmd, body=%wide.region_6.8_spmd.sunk | while | flops 101257736 | bytes 2312371 | solution.py:57
  227.7 2.4 fusion.71
  230.3 2.4 fusion.71
  232.8 2.4 fusion.71
  235.3 2.4 fusion.71
  237.8 0.7 convert_convert_fusion
  238.5 1.6 broadcast_multiply_fusion
  240.0 24.7 %while.29 = (s32[]{:T(128)}, f32[8,48]{1,0:T(8,128)S(1)}, f32[8,48,256]{2,1,0:T(8,128)}, s32[8]{0:T(128)S(1)}, bf16[8,2048,512]{2,1,0:T(8,128)(2,1)}, /*index=5*...) while((s32[]{:T(128)}, f32[8,48]{1,0:T(8,128)S(1)}, ...), condition=%wide.region_11.12_spmd, body=%wide.region_9.11_spmd.sunk | while | flops 202609152 | bytes 5983967 | solution.py:77
  240.1 3.1 fusion.75
  243.3 3.0 fusion.76
  246.3 3.1 fusion.75
  249.4 3.0 fusion.76
  252.5 3.1 fusion.75
  255.6 3.0 fusion.76
  258.7 3.1 fusion.75
  261.8 3.0 fusion.76
  264.8 1.8 divide_convert_fusion
  266.6 1.7 reshape.93
  268.3 11.8 %copy.19 = bf16[1,8,12288]{1,0,2:T(2,128)(2,1)} copy(bf16[1,8,12288]{2,1,0:T(8,128)(2,1)} %reshape.93) | data formatting | bytes 393216 | tf_op jit(solution)/shard_map/reshape | solution.py:112
  280.6 68.7 %reduce.1 = bf16[12288,8]{1,0:T(8,128)(2,1)} reduce(bf16[12288,1,8]{2,1,0:T(2,128)(2,1)} %bitcast.49, bf16[]{:T(256)} %broadcast.99), dimensions={1}, to_apply=%bitcast.31.reduce_sub_computation | reduce | bytes 393218
  349.3 5.6 %reshape.98 = bf16[16,2,3072]{2,1,0:T(2,128)(2,1)} reshape(bf16[12288,8]{1,0:T(8,128)(2,1)} %reduce.1) | data formatting | bytes 393216
  354.9 15.3 %all_to_all.33 = bf16[16,2,3072]{2,1,0:T(2,128)(2,1)} all-to-all(bf16[16,2,3072]{2,1,0:T(2,128)(2,1)} %reshape.98), channel_id=1, replica_groups=mesh['row'=8,'col'=16] {'col'}, dimensions={0} | all-to-all | bytes 393216 | tf_op jit(solution)/shard_map/all_to_all | solution.py:113
  370.2 11.7 %reshape.99 = bf16[12288,1,8]{2,1,0:T(2,128)(2,1)} reshape(bf16[16,2,3072]{2,1,0:T(2,128)(2,1)} %all_to_all.33) | data formatting | bytes 393216
  381.9 12.4 %copy.20 = bf16[1,8,12288]{2,1,0:T(8,128)(2,1)} copy(bf16[1,8,12288]{1,0,2:T(2,128)(2,1)} %bitcast.50) | data formatting | bytes 393216 | tf_op jit(solution)/shard_map/all_to_all | solution.py:113
  394.3 1.0 copy.32
  395.3 0.7 copy.33
  396.1 21.8 %all-gather.5.cloned.1.call-done = bf16[1024,768]{1,0:T(8,128)(2,1)} async-done(((bf16[128,768]{1,0:T(8,128)(2,1)}), bf16[1024,768]{1,0:T(8,128)(2,1)}) %all-gather.5.cloned.1.call-update) | async-done | bytes 1572880 | tf_op jit(solution)/shard_map/all_gather | solution.py:116
  417.9 6.9 %convolution_convert_fusion = bf16[1024,2304]{0,1:T(8,128)(2,1)} fusion(bf16[1024,768]{1,0:T(8,128)(2,1)} %all-gather.5.cloned.1.call-done, bf16[768,2304]{1,0:T(8,128)(2,1)S(1)} %copy-done), kind=kOutput, calls=%fused_computation.24 | convolution fusion | flops 3626237952 | bytes 9830400 | tf_op jit(solution)/shard_map/dot_general | solution.py:115
  424.9 80.3 %reduce-scatter.8.cloned.1.call-done = bf16[1024,144]{0,1:T(8,128)(2,1)} async-done(((bf16[1024,2304]{0,1:T(8,128)(2,1)}), bf16[1024,144]{0,1:T(8,128)(2,1)}) %reduce-scatter.8.cloned.1.call-update) | async-done | bytes 294928 | tf_op jit(solution)/shard_map/reduce_scatter | solution.py:120
  (45 shorter events, 1.8 us)
Async XLA Ops:
  7.2 410.8 %copy-start = (bf16[768,2304]{1,0:T(8,128)(2,1)S(1)}, bf16[768,2304]{1,0:T(8,128)(2,1)}, u32[]{:S(2)}) copy-start(bf16[768,2304]{1,0:T(8,128)(2,1)} %param.15) | copy-start | bytes 10616836
  7.2 122.8 %all-gather.3.cloned.1.call-start = ((), (), s32[]{:S(2)}) async-start(), calls=%async_computation.5 | async-start | bytes 5013504 | tf_op jit(solution)/shard_map/all_gather | solution.py:95
  138.8 47.8 %all-to-all-start = ((f32[8,16,8,768]{3,2,0,1:T(8,128)}), f32[8,16,8,768]{3,2,0,1:T(8,128)}, u32[]{:S(2)}, u32[]{:S(2)}) async-start(f32[8,16,8,768]{3,2,0,1:T(8,128)} %copy.14), calls=%async_computation | async-start | bytes 6291456 | tf_op jit(solution)/shard_map/all_to_all | solution.py:101
  144.1 46.6 %reduce-scatter.6.cloned.1.call-start = ((), (), s32[]{:S(2)}) async-start(), calls=%async_computation.7 | async-start | bytes 147456 | tf_op jit(solution)/shard_map/reduce_scatter | solution.py:104
  153.9 71.2 %reduce-scatter.4.cloned.1.call-start = ((), (), s32[]{:S(2)}) async-start(), calls=%async_computation.6 | async-start | bytes 3538944 | tf_op jit(solution)/shard_map/reduce_scatter | solution.py:103
  190.5 36.6 %copy-start.1 = (s32[8]{0:T(128)S(1)}, s32[8]{0:T(128)}, u32[]{:S(2)}) copy-start(s32[8]{0:T(128)} %param.17) | copy-start | bytes 100
  190.5 227.4 %all-gather.5.cloned.1.call-start = ((), (), s32[]{:S(2)}) async-start(), calls=%async_computation.8 | async-start | bytes 1769472 | tf_op jit(solution)/shard_map/all_gather | solution.py:116
  191.5 0.6 copy-start.2
  227.0 0.6 copy-start.3
  396.1 109.1 %reduce-scatter.8.cloned.1.call-start = ((), (), s32[]{:S(2)}) async-start(), calls=%async_computation.9 | async-start | bytes 5013504 | tf_op jit(solution)/shard_map/reduce_scatter | solution.py:120
Sparse Core Ops, SparseCore 0:
  78.3 51.6 all-gather.2
  154.1 29.3 reduce-scatter.5
  190.6 34.4 reduce-scatter.3
  396.2 21.7 all-gather.4
  425.0 80.1 reduce-scatter.7
where the time goes:
time: 515 us; the launch traced here: 512 us
  waiting for transfers between devices  219 us (43%)
  blocking collectives  81.9 us (16%)
  other arithmetic  80 us (16%)
  local copies, waits for them, and re-layouts  60 us (12%)
  matrix products  51 us (10%)
  between operations  13.8 us (3%)
  starting transfers between devices  5.69 us (1%)
    reduce_scatter x1, waiting for transfers between devices, shards(): lax.psum_scatter(out_term.astype(jnp.bfloat16), 'col', scatter_dimension=...  80.3 us
    unnamed x1, other arithmetic  68.7 us
    psum x1, blocking collectives, shards(): lax.psum((jnp.sum(floats, axis=1), jnp.sum(floats * floats, axis=1)), ('r...  66.7 us
    all_gather x1, waiting for transfers between devices, shards(): portion = lax.all_gather(normed, 'col', axis=1, tiled=True)  51.8 us
    all_to_all x1, waiting for transfers between devices, shards(): lax.all_to_all(query_four, 'col', split_axis=1, concat_axis=3, tiled=True)  32.6 us
    reduce_scatter x1, waiting for transfers between devices, shards(): lax.psum_scatter(moved, 'row', scatter_dimension=0, tiled=True)  32.5 us
    dot_general x8, matrix products, block_scores(): jnp.einsum('mqg,mfg->mqf', queries, kv_block[:, :, :head_dim], preferred_...  22.2 us
    all_gather x1, waiting for transfers between devices, shards(): lax.all_gather(returned, 'row', axis=0, tiled=True)  21.8 us
  transfers between devices with their start and end apart: 6, of which 5 were waited for; matrix products, arithmetic and copies ran while one was open for 3% of the time, Pallas kernels for 0%

commit v1 on v0

v1 whole, which is shorter than its diff:
```python
import functools

import jax
import jax.numpy as jnp
from jax import lax
from jax.experimental import pallas as pl
from jax.experimental.pallas import tpu as pltpu
from jax.sharding import PartitionSpec as P

MESH = pl.DeviceIdType.MESH
EPSILON = 1e-05
NEGATIVE_FLOOR = -1e30
HD = 256
SIDE = 4
VMEM_BYTES = 56 * 1024 * 1024


def rcopy(src, dst, send_sem, recv_sem, device):
    return pltpu.make_async_remote_copy(
        src_ref=src,
        dst_ref=dst,
        send_sem=send_sem,
        recv_sem=recv_sem,
        device_id=device,
        device_id_type=MESH,
    )


def along(ax, x, z, step):
    if ax == 0:
        return ((x + step + SIDE) % SIDE) * SIDE + z
    return x * SIDE + (z + step + SIDE) % SIDE


def loop(low, high, body):
    def step(i, carry):
        body(i)
        return carry

    lax.fori_loop(low, high, step, 0)


def greet(peers):
    barrier = pltpu.get_barrier_semaphore()
    count = 0
    for number, device_of in peers:

        def hello(d, device_of=device_of):
            pl.semaphore_signal(barrier, inc=1, device_id=device_of(d), device_id_type=MESH)

        loop(0, number, hello)
        count += number
    pl.semaphore_wait(barrier, count)


def project_kernel(
    n_features,
    tok,
    gain,
    wq,
    wkv,
    q_out,
    kv_out,
    xbuf,
    wbuf,
    gexp,
    xn,
    part,
    psend,
    own,
    qs,
    qrecv,
    stx,
    stz,
    sty,
    stc,
    smsg,
    zmsg,
    ymsg,
    cmsg,
    mi,
    w_sem,
    gs,
    gr,
    ps,
    pr,
    qsem,
    qrsem,
    sts,
    str_,
):
    r, c = lax.axis_index("row"), lax.axis_index("col")
    x, z = c // SIDE, c % SIDE
    y, core = r // 2, r % 2
    chunks, feats, lanes = tok.shape
    half = 80
    head_cols = wq.shape[1]
    n_col = SIDE * SIDE

    load_q = pltpu.make_async_copy(wq, wbuf.at[:, pl.ds(0, head_cols)], w_sem.at[0])
    load_kv = pltpu.make_async_copy(
        wkv.at[:, pl.ds(pl.multiple_of(x * 128, 128), 128)],
        wbuf.at[:, pl.ds(head_cols, 128)],
        w_sem.at[1],
    )
    load_q.start()
    load_kv.start()

    sums, squares = [], []
    for k in range(chunks):
        t = tok[k].astype(jnp.float32)
        sums.append(jnp.sum(t, axis=0, keepdims=True))
        squares.append(jnp.sum(t * t, axis=0, keepdims=True))
    smsg[0:8] = jnp.concatenate(sums, axis=0)
    smsg[8:16] = jnp.concatenate(squares, axis=0)
    smsg[16:24] = gain[...]
    stx[x] = smsg[...]

    def keep(j):
        xbuf[j, x, z] = tok[(r + 1 + j) % chunks]

    loop(0, chunks, keep)

    greet(
        [
            (n_col - 1, lambda d: (r, (c + 1 + d) % n_col)),
            (chunks - 1, lambda d: ((r + 1 + d) % chunks, c)),
        ]
    )

    def stat_x(d):
        return rcopy(smsg, stx.at[x], sts.at[d], str_.at[d], (r, along(0, x, z, d + 1)))

    def stat_z(d):
        return rcopy(zmsg, stz.at[z], sts.at[3 + d], str_.at[3 + d], (r, along(1, x, z, d + 1)))

    def stat_y(d):
        return rcopy(ymsg, sty.at[y], sts.at[6 + d], str_.at[6 + d], ((r + 2 * d + 2) % 8, c))

    stat_c = rcopy(cmsg, stc.at[core], sts.at[9], str_.at[9], (r + 1 - 2 * core, c))

    loop(0, 3, lambda d: stat_x(d).start())

    def block(ax, j, i):
        return xbuf.at[j, (i + SIDE) % SIDE, z] if ax == 0 else xbuf.at[j, x, (i + SIDE) % SIDE]

    def rows_of(ref, si):
        return ref.at[pl.ds(0, half)] if si == 0 else ref.at[pl.ds(half, feats - half)]

    def group(ax, j, i, low, n):
        i = (i + SIDE) % SIDE
        return xbuf.at[j, pl.ds(low, n), i] if ax == 0 else xbuf.at[j, i, pl.ds(low, n)]

    def first(ax, j, si):
        s = 1 - 2 * si
        here = block(ax, j, x if ax == 0 else z)
        return rcopy(here, here, gs.at[j, si], gr.at[j, si], (r, along(ax, x, z, s)))

    def first_on(ax, j, si):
        s = 1 - 2 * si
        ref = rows_of(block(ax, j, (x if ax == 0 else z) - s), si)
        return rcopy(ref, ref, gs.at[j, 2 + si], gr.at[j, 2 + si], (r, along(ax, x, z, s)))

    def second(ax, j, si):
        s = 1 - 2 * si
        ref = group(ax, j, z if ax == 0 else x, 0, SIDE)
        return rcopy(ref, ref, gs.at[j, 4 + si], gr.at[j, 4 + si], (r, along(1 - ax, x, z, s)))

    def second_on(ax, j, si):
        s = 1 - 2 * si
        ref = group(ax, j, (z if ax == 0 else x) - s, 2 * si, 2)
        return rcopy(ref, ref, gs.at[j, 6 + si], gr.at[j, 6 + si], (r, along(1 - ax, x, z, s)))

    def both(p, do):
        for si in (0, 1):
            for ax in (0, 1):
                do(ax, 2 * p + ax, si)

    pairs = chunks // 2
    loop(0, pairs, lambda p: both(p, lambda ax, j, si: first(ax, j, si).start()))

    loop(0, 3, lambda d: stat_x(d).wait_recv())
    zmsg[0:16] = stx[0, 0:16] + stx[1, 0:16] + stx[2, 0:16] + stx[3, 0:16]
    for i in range(SIDE):
        zmsg[16 + 8 * i : 24 + 8 * i] = stx[i, 16:24]
    stz[z] = zmsg[...]
    loop(0, 3, lambda d: stat_z(d).start())

    def forward(p):
        def do(ax, j, si):
            first(ax, j, si).wait_recv()
            first_on(ax, j, si).start()

        both(p, do)

    loop(0, pairs, forward)

    def start_second(p):
        both(p, lambda ax, j, si: first_on(ax, j, si).wait_recv())
        both(p, lambda ax, j, si: second(ax, j, si).start())

    loop(0, 2, start_second)

    loop(0, 3, lambda d: stat_z(d).wait_recv())
    ymsg[...] = stz[0, 0:16] + stz[1, 0:16] + stz[2, 0:16] + stz[3, 0:16]
    sty[y] = ymsg[...]
    loop(0, 3, lambda d: stat_y(d).start())

    def spread(i):
        rows = stz[i % SIDE, pl.ds(pl.multiple_of(16 + 8 * (i // SIDE), 8), 8)]
        gexp[i, 0:128] = jnp.broadcast_to(rows[0:1], (128, 128)).T
        gexp[i, 128:feats] = jnp.broadcast_to(rows[1:2], (128, 128)).T[0 : feats - 128]

    loop(0, n_col, spread)

    loop(0, 3, lambda d: stat_y(d).wait_recv())
    cmsg[...] = sty[0] + sty[1] + sty[2] + sty[3]
    stc[core] = cmsg[...]
    stat_c.start()
    stat_c.wait_recv()
    total = stc[0] + stc[1]
    average = total[0:8] / n_features
    mi[0:8] = average
    mi[8:16] = lax.rsqrt(total[8:16] / n_features - average * average + EPSILON)

    load_q.wait()
    load_kv.wait()

    def partial_send(j):
        return rcopy(psend.at[j], part.at[j], ps.at[j], pr.at[j], ((r + 1 + j) % chunks, c))

    def compute(j):
        k = (r + 1 + j) % chunks
        mean, inverse = mi[pl.ds(k, 1), :], mi[pl.ds(8 + k, 1), :]
        for i in range(n_col):
            t = xbuf[j, i // SIDE, i % SIDE].astype(jnp.float32)
            xn[feats * i : feats * (i + 1)] = ((t - mean) * inverse * gexp[i]).astype(jnp.bfloat16)
        return lax.dot_general(
            xn[...], wbuf[...], (((0,), (0,)), ((), ())), preferred_element_type=jnp.float32
        )

    def pair(p):
        @pl.when(p < pairs - 2)
        def _():
            start_second(p + 2)

        def do(ax, j, si):
            second(ax, j, si).wait_recv()
            second_on(ax, j, si).start()

        both(p, do)
        both(p, lambda ax, j, si: second_on(ax, j, si).wait_recv())

        def one(i):
            j = 2 * p + i
            own[...] = compute(j)

            @pl.when(j < chunks - 1)
            def _():
                psend[j] = own[...].astype(jnp.bfloat16)
                partial_send(j).start()

        loop(0, 2, one)

    loop(0, pairs, pair)

    loop(0, chunks - 1, lambda j: partial_send(j).wait_recv())
    acc = own[...]
    for j in range(chunks - 1):
        acc = acc + part[j].astype(jnp.float32)
    for i in range(qs.shape[0]):
        qs[i] = acc[:, 128 * i : 128 * (i + 1)]

    rows_dev = q_out.shape[0]

    def row_send(d):
        to = (c + 1 + d) % n_col
        return rcopy(
            qs.at[:, pl.ds(pl.multiple_of(to * rows_dev, 8), rows_dev)],
            qrecv.at[:, pl.ds(pl.multiple_of(c * rows_dev, 8), rows_dev)],
            qsem.at[d],
            qrsem.at[d],
            (r, to),
        )

    loop(0, n_col - 1, lambda d: row_send(d).start())
    mine = pl.ds(pl.multiple_of(c * rows_dev, 8), rows_dev)
    qrecv[:, mine] = qs[:, mine]
    loop(0, n_col - 1, lambda d: row_send(d).wait_recv())
    for b in range(rows_dev):
        for i in range(head_cols // 128):
            at = slice(n_col * (i // 2), n_col * (i // 2 + 1))
            q_out[b, at, 128 * (i % 2) : 128 * (i % 2 + 1)] = qrecv[
                i, pl.ds(b, n_col, stride=rows_dev)
            ].astype(jnp.bfloat16)
    for i in range(SIDE):
        kv_out[:, 128 * i : 128 * (i + 1)] = qrecv[
            head_cols // 128, 8 * SIDE * i : 8 * SIDE * i + 8
        ].astype(jnp.bfloat16)

    loop(0, 3, lambda d: stat_x(d).wait_send())
    loop(0, 3, lambda d: stat_z(d).wait_send())
    loop(0, 3, lambda d: stat_y(d).wait_send())
    stat_c.wait_send()

    def sent(p):
        for send in (first, first_on, second, second_on):
            both(p, lambda ax, j, si: send(ax, j, si).wait_send())

    loop(0, pairs, sent)
    loop(0, chunks - 1, lambda j: partial_send(j).wait_send())
    loop(0, n_col - 1, lambda d: row_send(d).wait_send())


def project(tokens, gain, query_weight, kv_weight, n_features, heads, rows_dev):
    chunks, feats, lanes = tokens.shape
    depth, head_cols = query_weight.shape
    wide = head_cols + 128
    n_col = SIDE * SIDE
    f32, bf16 = jnp.float32, jnp.bfloat16
    vmem = pl.BlockSpec(memory_space=pltpu.VMEM)
    anywhere = pl.BlockSpec(memory_space=pl.ANY)
    dma = pltpu.SemaphoreType.DMA
    return pl.pallas_call(
        functools.partial(project_kernel, n_features),
        out_shape=(
            jax.ShapeDtypeStruct((rows_dev, heads, HD), bf16),
            jax.ShapeDtypeStruct((rows_dev, kv_weight.shape[1]), bf16),
        ),
        in_specs=[vmem, vmem, anywhere, anywhere],
        out_specs=(vmem, vmem),
        scratch_shapes=[
            pltpu.VMEM((chunks, SIDE, SIDE, feats, lanes), bf16),
            pltpu.VMEM((depth, wide), bf16),
            pltpu.VMEM((n_col, feats, lanes), f32),
            pltpu.VMEM((depth, lanes), bf16),
            pltpu.VMEM((chunks - 1, lanes, wide), bf16),
            pltpu.VMEM((chunks - 1, lanes, wide), bf16),
            pltpu.VMEM((lanes, wide), f32),
            pltpu.VMEM((wide // 128, lanes, 128), f32),
            pltpu.VMEM((wide // 128, lanes, 128), f32),
            pltpu.VMEM((SIDE, 24, lanes), f32),
            pltpu.VMEM((SIDE, 48, lanes), f32),
            pltpu.VMEM((SIDE, 16, lanes), f32),
            pltpu.VMEM((2, 16, lanes), f32),
            pltpu.VMEM((24, lanes), f32),
            pltpu.VMEM((48, lanes), f32),
            pltpu.VMEM((16, lanes), f32),
            pltpu.VMEM((16, lanes), f32),
            pltpu.VMEM((16, lanes), f32),
            dma((2,)),
            dma((chunks, 8)),
            dma((chunks, 8)),
            dma((chunks - 1,)),
            dma((chunks - 1,)),
            dma((n_col - 1,)),
            dma((n_col - 1,)),
            dma((10,)),
            dma((10,)),
        ],
        compiler_params=pltpu.CompilerParams(
            collective_id=0, has_side_effects=True, vmem_limit_bytes=VMEM_BYTES
        ),
        name="project",
    )(tokens, gain, query_weight, kv_weight)


def attend_kernel(lengths, q_ref, kv_ref, cache, out):
    b = pl.program_id(0)
    rows_dev = pl.num_programs(0)
    positions = cache.shape[1]
    scale = HD**-0.5
    q = q_ref[0]
    fresh = kv_ref[pl.ds(b, 1), :]
    new_key, new_value = fresh[:, :HD], fresh[:, HD:]
    scores = (
        lax.dot_general(
            q, cache[0, :, :HD], (((1,), (1,)), ((), ())), preferred_element_type=jnp.float32
        )
        * scale
    )
    position = lax.broadcasted_iota(jnp.int32, (1, positions), 1)
    scores = jnp.where(position < lengths[b], scores, NEGATIVE_FLOOR)
    new_score = jnp.sum(q.astype(jnp.float32) * new_key, axis=1, keepdims=True) * scale
    top = jnp.maximum(jnp.max(scores, axis=1, keepdims=True), new_score)
    weights = jnp.exp(scores - top)
    new_weight = jnp.exp(new_score - top)
    total = jnp.sum(weights, axis=1, keepdims=True) + new_weight
    context = jnp.dot(
        weights.astype(jnp.bfloat16), cache[0, :, HD:], preferred_element_type=jnp.float32
    )
    context = context + new_weight.astype(jnp.bfloat16).astype(jnp.float32) * new_value
    context = context / total
    n_col = SIDE * SIDE
    for i in range(out.shape[0]):
        out[i, pl.ds(b, n_col, stride=8)] = context[
            n_col * (i // 2) : n_col * (i // 2 + 1), 128 * (i % 2) : 128 * (i % 2 + 1)
        ]


def attend(lengths, queries, new_kv, cache):
    rows_dev, heads, _ = queries.shape
    positions, wide = cache.shape[1:]
    n_col = SIDE * SIDE
    cols = heads // n_col * HD
    return pl.pallas_call(
        attend_kernel,
        grid_spec=pltpu.PrefetchScalarGridSpec(
            num_scalar_prefetch=1,
            grid=(rows_dev,),
            in_specs=[
                pl.BlockSpec((1, heads, HD), lambda b, _: (b, 0, 0)),
                pl.BlockSpec((rows_dev, wide), lambda b, _: (0, 0)),
                pl.BlockSpec((1, positions, wide), lambda b, _: (b, 0, 0)),
            ],
            out_specs=pl.BlockSpec((cols // 128, n_col * rows_dev, 128), lambda b, _: (0, 0, 0)),
        ),
        out_shape=jax.ShapeDtypeStruct((cols // 128, n_col * rows_dev, 128), jnp.float32),
        compiler_params=pltpu.CompilerParams(vmem_limit_bytes=VMEM_BYTES),
        name="attend",
    )(lengths, queries, new_kv, cache)


def output_kernel(
    ctx, wo, out, wbuf, crecv, allctx, pbuf, r1a, r1b, r2a, r2b, w_sem, cs, cr, ys, yr, gs, gr
):
    r, c = lax.axis_index("row"), lax.axis_index("col")
    x, z = c // SIDE, c % SIDE
    core = r % 2
    partner = r + 1 - 2 * core
    chunks, feats, lanes = out.shape
    half = 80
    n_col = SIDE * SIDE
    rows_dev = ctx.shape[1] // n_col

    load = pltpu.make_async_copy(wo, wbuf, w_sem)
    load.start()
    greet(
        [
            (n_col - 1, lambda d: (r, (c + 1 + d) % n_col)),
            (1, lambda d: (partner, c)),
            (3, lambda d: ((r + 2 * d + 2) % chunks, c)),
        ]
    )

    def row_send(d):
        to = (c + 1 + d) % n_col
        return rcopy(
            ctx.at[:, pl.ds(pl.multiple_of(to * rows_dev, 8), rows_dev)],
            crecv.at[:, pl.ds(pl.multiple_of(c * rows_dev, 8), rows_dev)],
            cs.at[d],
            cr.at[d],
            (r, to),
        )

    loop(0, n_col - 1, lambda d: row_send(d).start())
    mine = pl.ds(pl.multiple_of(c * rows_dev, 8), rows_dev)
    crecv[:, mine] = ctx[:, mine]
    loop(0, n_col - 1, lambda d: row_send(d).wait_recv())
    for i in range(crecv.shape[0]):
        allctx[0, :, 128 * i : 128 * (i + 1)] = crecv[i].astype(jnp.bfloat16)

    def y_send(d):
        step = jnp.where(d == 0, chunks - 2, jnp.where(d == 1, 2, 4))
        return rcopy(
            allctx.at[0], allctx.at[2 + 2 * d], ys.at[d], yr.at[d], ((r + step) % chunks, c)
        )

    def pass_on(d):
        return rcopy(
            allctx.at[2 + 2 * d], allctx.at[3 + 2 * d], ys.at[3 + d], yr.at[3 + d], (partner, c)
        )

    to_partner = rcopy(allctx.at[0], allctx.at[1], ys.at[6], yr.at[6], (partner, c))
    to_partner.start()
    loop(0, 3, lambda d: y_send(d).start())
    load.wait()

    def place(ax, i):
        return (i + SIDE) % SIDE

    def mid(ax):
        return x if ax == 0 else z

    def end(ax):
        return z if ax == 0 else x

    def group(ax, j, i, low, n):
        i = (i + SIDE) % SIDE
        return pbuf.at[j, i, pl.ds(low, n)] if ax == 0 else pbuf.at[j, pl.ds(low, n), i]

    def block(ax, j, i):
        i = (i + SIDE) % SIDE
        return pbuf.at[j, x, i] if ax == 0 else pbuf.at[j, i, z]

    def rows_of(ref, si):
        return ref.at[pl.ds(0, half)] if si == 0 else ref.at[pl.ds(half, feats - half)]

    def send_1a(ax, j, si):
        s = 1 - 2 * si
        return rcopy(
            group(ax, j, mid(ax) + 2, 2 * si, 2),
            r1a.at[j, si],
            gs.at[j, si],
            gr.at[j, si],
            (r, along(ax, x, z, s)),
        )

    def send_1b(ax, j, si):
        s = 1 - 2 * si
        return rcopy(
            group(ax, j, mid(ax) + s, 0, SIDE),
            r1b.at[j, si],
            gs.at[j, 2 + si],
            gr.at[j, 2 + si],
            (r, along(ax, x, z, s)),
        )

    def send_2a(ax, j, si):
        s = 1 - 2 * si
        return rcopy(
            rows_of(block(ax, j, end(ax) + 2), si),
            rows_of(r2a.at[j], si),
            gs.at[j, 4 + si],
            gr.at[j, 4 + si],
            (r, along(1 - ax, x, z, s)),
        )

    def send_2b(ax, j, si):
        s = 1 - 2 * si
        return rcopy(
            block(ax, j, end(ax) + s),
            r2b.at[j, si],
            gs.at[j, 6 + si],
            gr.at[j, 6 + si],
            (r, along(1 - ax, x, z, s)),
        )

    def both(p, do):
        for ax in (0, 1):
            do(ax, 2 * p + ax)

    def add_into(ref, *terms):
        total = ref[...].astype(jnp.float32)
        for term in terms:
            total = total + term[...].astype(jnp.float32)
        ref[...] = total.astype(jnp.bfloat16)

    def stage_1b(ax, j):
        for si in (0, 1):
            s = 1 - 2 * si
            send_1a(ax, j, si).wait_recv()
            add_into(group(ax, j, mid(ax) + s, 2 * si, 2), r1a.at[j, si])
            send_1b(ax, j, si).start()

    def stage_2a(ax, j):
        send_1b(ax, j, 0).wait_recv()
        send_1b(ax, j, 1).wait_recv()
        add_into(group(ax, j, mid(ax), 0, SIDE), r1b.at[j, 0], r1b.at[j, 1])
        for si in (0, 1):
            send_2a(ax, j, si).start()

    def stage_2b(ax, j):
        for si in (0, 1):
            s = 1 - 2 * si
            send_2a(ax, j, si).wait_recv()
            add_into(rows_of(block(ax, j, end(ax) + s), si), rows_of(r2a.at[j], si))
            send_2b(ax, j, si).start()

    def owner(j):
        step = jnp.where(j < 4, j // 2, jnp.where(j < 6, 3, 2))
        row = (r // 2 + step) % (chunks // 2)
        return 2 * row + (core + j) % 2

    def stage_end(ax, j):
        send_2b(ax, j, 0).wait_recv()
        send_2b(ax, j, 1).wait_recv()
        total = (
            block(ax, j, end(ax))[...].astype(jnp.float32)
            + r2b[j, 0].astype(jnp.float32)
            + r2b[j, 1].astype(jnp.float32)
        )
        out[owner(j)] = total.astype(jnp.bfloat16)

    def compute(j):
        term = jnp.dot(allctx[j], wbuf[...], preferred_element_type=jnp.float32)
        turned = term.astype(jnp.bfloat16).T
        for i in range(n_col):
            pbuf[j, i // SIDE, i % SIDE] = turned[feats * i : feats * (i + 1)]

    pairs = chunks // 2

    def step(t):
        @pl.when(t >= 4)
        def _():
            both(t - 4, stage_end)

        @pl.when(jnp.logical_and(t >= 3, t < pairs + 3))
        def _():
            both(t - 3, stage_2b)

        @pl.when(jnp.logical_and(t >= 2, t < pairs + 2))
        def _():
            both(t - 2, stage_2a)

        @pl.when(jnp.logical_and(t >= 1, t < pairs + 1))
        def _():
            both(t - 1, stage_1b)

        @pl.when(t < pairs)
        def _():
            compute(2 * t)
            for si in (0, 1):
                send_1a(0, 2 * t, si).start()

            @pl.when(t == 0)
            def _():
                to_partner.wait_recv()

            @pl.when(t > 0)
            def _():
                pass_on(t - 1).wait_recv()

            compute(2 * t + 1)
            for si in (0, 1):
                send_1a(1, 2 * t + 1, si).start()

        @pl.when(t < pairs - 1)
        def _():
            y_send(t).wait_recv()
            pass_on(t).start()

    loop(0, pairs + 4, step)

    def sent(p):
        for si in (0, 1):
            for send in (send_1a, send_1b, send_2a, send_2b):
                both(p, lambda ax, j: send(ax, j, si).wait_send())

    loop(0, pairs, sent)
    loop(0, n_col - 1, lambda d: row_send(d).wait_send())
    loop(0, 3, lambda d: y_send(d).wait_send())
    loop(0, 3, lambda d: pass_on(d).wait_send())
    to_partner.wait_send()


def project_out(context, weight, chunks, feats):
    rows, cols = context.shape[1], context.shape[0] * 128
    lanes = rows
    f32, bf16 = jnp.float32, jnp.bfloat16
    vmem = pl.BlockSpec(memory_space=pltpu.VMEM)
    anywhere = pl.BlockSpec(memory_space=pl.ANY)
    dma = pltpu.SemaphoreType.DMA
    n_col = SIDE * SIDE
    return pl.pallas_call(
        output_kernel,
        out_shape=jax.ShapeDtypeStruct((chunks, feats, lanes), bf16),
        in_specs=[vmem, anywhere],
        out_specs=vmem,
        scratch_shapes=[
            pltpu.VMEM(weight.shape, bf16),
            pltpu.VMEM(context.shape, f32),
            pltpu.VMEM((chunks, rows, cols), bf16),
            pltpu.VMEM((chunks, SIDE, SIDE, feats, lanes), bf16),
            pltpu.VMEM((chunks, 2, 2, feats, lanes), bf16),
            pltpu.VMEM((chunks, 2, SIDE, feats, lanes), bf16),
            pltpu.VMEM((chunks, feats, lanes), bf16),
            pltpu.VMEM((chunks, 2, feats, lanes), bf16),
            dma,
            dma((n_col - 1,)),
            dma((n_col - 1,)),
            dma((7,)),
            dma((7,)),
            dma((chunks, 8)),
            dma((chunks, 8)),
        ],
        compiler_params=pltpu.CompilerParams(
            collective_id=1, has_side_effects=True, vmem_limit_bytes=VMEM_BYTES
        ),
        name="project_out",
    )(context, weight)


def shards(
    tokens, layer_norm_gain, query_weight, kv_weight, output_weight_matrix, kv_cache, lengths
):
    chunks = lax.axis_size("row")
    devices = chunks * lax.axis_size("col")
    rows, feats = tokens.shape
    rows_dev = kv_cache.shape[0]
    heads = query_weight.shape[1] * lax.axis_size("col") // HD
    lanes = rows // chunks
    turned = tokens.reshape(chunks, lanes, feats).transpose(0, 2, 1)
    gain = jnp.pad(layer_norm_gain.astype(jnp.float32), (0, 8 * 128 - feats)).reshape(8, 128)
    queries, new_kv = project(
        turned, gain, query_weight, kv_weight, feats * devices, heads, rows_dev
    )
    context = attend(lengths, queries, new_kv.astype(jnp.float32), kv_cache)
    branch = project_out(context, output_weight_matrix, chunks, feats)
    branch = branch.transpose(0, 2, 1).reshape(rows, feats)
    return (branch, new_kv)


def solution(mesh):
    placed = (
        P(None, ("row", "col")),
        P(("row", "col")),
        P("row", "col"),
        P("row", None),
        P("col", "row"),
        P(("row", "col"), None, None),
        P(("row", "col")),
    )
    return jax.shard_map(
        shards,
        mesh=mesh,
        in_specs=placed,
        out_specs=(P(None, ("row", "col")), P(("row", "col"), None)),
        check_vma=False,
    )
```

time: 515 us -> 145 us (0.28)
  waiting for transfers between devices: 219 us -> 0 us
  Pallas kernels: 0 us -> 138 us
  blocking collectives: 81.9 us -> 0 us
  other arithmetic: 80 us -> 2.6 us
  local copies, waits for them, and re-layouts: 60 us -> 3.08 us
  matrix products: 51 us -> 0 us
  between operations: 13.8 us -> 0.66 us
  starting transfers between devices: 5.69 us -> 0 us
    pallas_call x0 -> x3, Pallas kernels: none -> 138 us  [the longest x1 63.7 us: project(): pl.pallas_call(functools.partial(project_kernel, n_features), out_shape=(...]
    reduce_scatter x3 -> x0, waiting for transfers between devices: 113 us -> none  [the longest x1 80.3 us: shards(): lax.psum_scatter(out_term.astype(jnp.bfloat16), 'col', scatter_dimension=...]
    all_gather x2 -> x0, waiting for transfers between devices: 73.7 us -> none  [the longest x1 51.8 us: shards(): portion = lax.all_gather(normed, 'col', axis=1, tiled=True)]
    unnamed x1 -> x0, other arithmetic: 68.7 us -> none
    psum x1 -> x0, blocking collectives: 66.7 us -> none  [shards(): lax.psum((jnp.sum(floats, axis=1), jnp.sum(floats * floats, axis=1)), ('r...]
    dot_general x16 -> x0, matrix products: 51 us -> none  [the longest x8 22.2 us: block_scores(): jnp.einsum('mqg,mfg->mqf', queries, kv_block[:, :, :head_dim], preferred_...]
    all_to_all x1 -> x0, waiting for transfers between devices: 32.6 us -> none  [shards(): lax.all_to_all(query_four, 'col', split_axis=1, concat_axis=3, tiled=True)]
    unnamed x12 -> x5, local copies, waits for them, and re-layouts: 20 us -> 0.61 us
  transfers between devices with their start and end apart: 6 -> 0, of which waited for: 5 -> 0; matrix products, arithmetic and copies ran while one was open for 3% -> 0% of each run, Pallas kernels for 0% -> 0%
where the time goes in v1:
time: 145 us
  Pallas kernels  138 us (95%)
  local copies, waits for them, and re-layouts  3.08 us (2%)
  other arithmetic  2.6 us (2%)
    pallas_call x1, Pallas kernels, project(): pl.pallas_call(functools.partial(project_kernel, n_features), out_shape=(...  63.7 us
    pallas_call x1, Pallas kernels, project_out(): pl.pallas_call(output_kernel, out_shape=jax.ShapeDtypeStruct((chunks, fea...  61.5 us
    pallas_call x1, Pallas kernels, attend(): pl.pallas_call(attend_kernel, grid_spec=pltpu.PrefetchScalarGridSpec(num_...  13.2 us

profile of v1, /device:TPU:8, one launch (start us, length us, event | category | flops | bytes accessed | tf_op | source)
XLA Modules:
  0.0 144.8 jit_solution(2280032439495599469)
XLA Ops:
  0.6 0.0 copy-start
  0.6 1.3 bitcast_convert_fusion.gain
  1.9 0.0 copy-done
  1.9 0.8 bitcast_bitcast_fusion.tok
  2.7 63.7 %project.1 = (bf16[8,48,256]{2,1,0:T(8,128)(2,1)}, bf16[8,512]{1,0:T(8,128)(2,1)}) custom-call(bf16[8,144,128]{2,1,0:T(8,128)(2,1)} %bitcast_bitcast_fusion.tok, f32[8,128]{1,0:T(8,128)} %bitcast_convert_fusion.gain, bf16[2304,768]{1,0:T(8,128)(2,1)} %wq.1, bf16[2304,512]{1,0:T(8,128)(2,1)} %wkv.1), custom_call_target="tpu_custom_call" | custom-call | tf_op jit(solution)/shard_map/project/pallas_call | solution.py:324
  66.4 1.3 convert_element_type.6.kv_ref
  67.7 13.2 %attend.1.ctx = f32[6,128,128]{2,1,0:T(8,128)} custom-call(s32[8]{0:T(128)} %lengths.1, bf16[8,48,256]{2,1,0:T(8,128)(2,1)} %get-tuple-element.4.q_ref, f32[8,512]{1,0:T(8,128)} %convert_element_type.6.kv_ref, bf16[8,2048,512]{2,1,0:T(8,128)(2,1)} %cache.1), custom_call_target="tpu_custom_call" | custom-call | tf_op jit(solution)/shard_map/attend/pallas_call | solution.py:406
  81.0 0.0 copy-start.1
  81.0 61.5 %project_out.1 = bf16[8,144,128]{2,1,0:T(8,128)(2,1)} custom-call(f32[6,128,128]{2,1,0:T(8,128)} %attend.1.ctx, bf16[768,2304]{1,0:T(8,128)(2,1)} %wo.1), custom_call_target="tpu_custom_call" | custom-call | tf_op jit(solution)/shard_map/project_out/pallas_call | solution.py:655
  142.5 1.7 %copy_bitcast_fusion = bf16[1024,144]{0,1:T(8,128)(2,1)} fusion(bf16[8,144,128]{2,1,0:T(8,128)(2,1)} %project_out.1), kind=kLoop, calls=%fused_computation | loop fusion | bytes 589824 | tf_op jit(solution)/shard_map/reshape | solution.py:700
  144.2 0.0 copy-done.1
  144.2 0.6 copy.16
Async XLA Ops:
  0.6 1.3 copy-start
  81.0 63.3 %copy-start.1 = (bf16[8,512]{1,0:T(8,128)(2,1)S(1)}, bf16[8,512]{1,0:T(8,128)(2,1)}, u32[]{:S(2)}) copy-start(bf16[8,512]{1,0:T(8,128)(2,1)} %get-tuple-element.9) | copy-start | bytes 24580

commit v2 on v0

v2 whole, which is shorter than its diff:
```python
import functools

import jax
import jax.numpy as jnp
from jax import lax
from jax.experimental import pallas as pl
from jax.experimental.pallas import tpu as pltpu
from jax.sharding import PartitionSpec as P

MESH = pl.DeviceIdType.MESH
EPSILON = 1e-05
NEGATIVE_FLOOR = -1e30
HD = 256
SIDE = 4
N_COL = SIDE * SIDE
N_ROW = 8
QUARTERS = 4
ROWS_DEV = 8
LANES = 128
CHUNKS = 2 * QUARTERS
HALF = 80
ORDER = [
    ("first", 2), ("first", 1), ("first", 3), ("st_x", 0), ("first", 0), ("first_on", 2),
    ("first_on", 1), ("first_on", 3), ("st_z", 0), ("second", 2), ("second", 1), ("first_on", 0),
    ("st_y", 0), ("st_c", 0), ("second_on", 2), ("second_on", 1), ("second", 0), ("second", 3),
    ("st_end", 0), ("project", 2), ("sum_cores", 2), ("project", 1), ("sum_cores", 1), ("second_on", 0),
    ("rows_out", 2), ("second_on", 3), ("project", 0), ("rows_out", 1), ("sum_cores", 0), ("project", 3),
    ("attend", 2), ("sum_cores", 3), ("rows_out", 0), ("attend", 1), ("contexts_out", 2), ("rows_out", 3),
    ("attend", 0), ("contexts_out", 1), ("contexts_on", 2), ("project_out", 2), ("attend", 3), ("contexts_out", 0),
    ("contexts_on", 1), ("project_out", 1), ("sum_1b", 2), ("contexts_out", 3), ("contexts_on", 0), ("project_out", 0),
    ("sum_1b", 1), ("contexts_on", 3), ("sum_2a", 2), ("project_out", 3), ("sum_1b", 0), ("sum_1b", 3),
    ("sum_2a", 1), ("sum_2b", 2), ("sum_2a", 0), ("sum_2a", 3), ("sum_2b", 1), ("sum_end", 2),
    ("sum_2b", 0), ("sum_2b", 3), ("sum_end", 1), ("sum_end", 0), ("sum_end", 3),
]
VMEM_BYTES = 60 * 1024 * 1024
F32, BF16 = jnp.float32, jnp.bfloat16


def rcopy(src, dst, send_sem, recv_sem, device):
    return pltpu.make_async_remote_copy(
        src_ref=src,
        dst_ref=dst,
        send_sem=send_sem,
        recv_sem=recv_sem,
        device_id=device,
        device_id_type=MESH,
    )


def along(ax, x, z, step):
    if ax == 0:
        return ((x + step + SIDE) % SIDE) * SIDE + z
    return x * SIDE + (z + step + SIDE) % SIDE


def loop(low, high, body):
    def step(i, carry):
        body(i)
        return carry

    lax.fori_loop(low, high, step, 0)


def greet(peers):
    barrier = pltpu.get_barrier_semaphore()
    count = 0
    for number, device_of in peers:

        def hello(d, device_of=device_of):
            pl.semaphore_signal(barrier, inc=1, device_id=device_of(d), device_id_type=MESH)

        loop(0, number, hello)
        count += number
    pl.semaphore_wait(barrier, count)


def rows_of(ref, si):
    feats = ref.shape[0]
    return ref.at[pl.ds(0, HALF)] if si == 0 else ref.at[pl.ds(HALF, feats - HALF)]


def both(s, do):
    for ax in (0, 1):
        do(ax, 2 * s + ax)


def add_into(ref, *terms):
    total = ref[...].astype(F32)
    for term in terms:
        total = total + term[...].astype(F32)
    ref[...] = total.astype(BF16)


def kernel(
    n_features,
    tok,
    gain,
    wq,
    wkv,
    wo,
    cache,
    lengths,
    out,
    kv_out,
    perm,
    xbuf,
    qw,
    ow,
    kvc,
    gexp,
    xn,
    pq,
    pqr,
    yq,
    yqr,
    slab,
    slabr,
    cslab,
    cslabr,
    fold,
    cfold,
    qt,
    kvf,
    allctx,
    pbuf,
    r1a,
    r1b,
    r2a,
    r2b,
    ot,
    stx,
    stz,
    sty,
    stc,
    smsg,
    zmsg,
    ymsg,
    cmsg,
    mi,
    w_sem,
    k_sem,
    gs,
    gr,
    os_,
    or_,
    ps,
    pr,
    as_,
    ar,
    cs,
    cr,
    ss,
    sr,
):
    r, c = lax.axis_index("row"), lax.axis_index("col")
    x, z = c // SIDE, c % SIDE
    y, core = r // 2, r % 2
    partner = r + 1 - 2 * core
    feats = tok.shape[0]
    head_cols = wq.shape[1]
    q_parts = head_cols // LANES
    wide_parts = q_parts + 1
    wide = wide_parts * LANES
    block_rows = LANES // 4

    load_q = pltpu.make_async_copy(wq, qw.at[:, pl.ds(0, head_cols)], w_sem.at[0])
    load_kv = pltpu.make_async_copy(
        wkv.at[:, pl.ds(pl.multiple_of(x * LANES, LANES), LANES)],
        qw.at[:, pl.ds(head_cols, LANES)],
        w_sem.at[1],
    )
    load_o = pltpu.make_async_copy(wo, ow, w_sem.at[2])
    load_q.start()
    load_kv.start()

    def load_cache(b):
        return pltpu.make_async_copy(cache.at[b], kvc.at[b], k_sem.at[b])

    row = lax.broadcasted_iota(jnp.int32, (4 * LANES, LANES), 0)
    lane = lax.broadcasted_iota(jnp.int32, (4 * LANES, LANES), 1)
    same = jnp.logical_and(
        row // LANES == lane // block_rows, row % LANES // ROWS_DEV == lane % N_COL
    )
    bit = lane % block_rows // N_COL
    for s in range(QUARTERS):
        hit = jnp.logical_and(same, row % ROWS_DEV == 2 * s + bit)
        perm[s] = jnp.where(hit, 1.0, 0.0).astype(BF16)

    sums, squares = [], []
    for j in range(CHUNKS):
        s, h = j // 2, j % 2
        t = jnp.dot(
            tok[:, 4 * LANES * h : 4 * LANES * (h + 1)], perm[s], preferred_element_type=F32
        )
        xbuf[j, x, z] = t.astype(BF16)
        sums.append(jnp.sum(t, axis=0, keepdims=True))
        squares.append(jnp.sum(t * t, axis=0, keepdims=True))
    smsg[0:8] = jnp.concatenate(sums, axis=0)
    smsg[8:16] = jnp.concatenate(squares, axis=0)
    gains = gain[...].astype(F32)
    smsg[16:24] = jnp.zeros((8, LANES), F32)
    smsg[16:17] = gains[:, 0:LANES]
    smsg[17:18, 0 : feats - LANES] = gains[:, LANES:feats]
    stx[x] = smsg[...]

    fold[...] = jnp.zeros_like(fold)
    cfold[...] = jnp.zeros_like(cfold)
    greet(
        [
            (N_COL - 1, lambda d: (r, (c + 1 + d) % N_COL)),
            (1, lambda d: (partner, c)),
            (3, lambda d: ((r + 2 * d + 2) % N_ROW, c)),
        ]
    )

    def stat_x(d):
        return rcopy(smsg, stx.at[x], ss.at[d], sr.at[d], (r, along(0, x, z, d + 1)))

    def stat_z(d):
        return rcopy(zmsg, stz.at[z], ss.at[3 + d], sr.at[3 + d], (r, along(1, x, z, d + 1)))

    def stat_y(d):
        return rcopy(ymsg, sty.at[y], ss.at[6 + d], sr.at[6 + d], ((r + 2 * d + 2) % N_ROW, c))

    stat_c = rcopy(cmsg, stc.at[core], ss.at[9], sr.at[9], (partner, c))

    def mid(ax):
        return x if ax == 0 else z

    def end(ax):
        return z if ax == 0 else x

    def gblock(ax, j, i):
        i = (i + SIDE) % SIDE
        return xbuf.at[j, i, z] if ax == 0 else xbuf.at[j, x, i]

    def ggroup(ax, j, i, low, n):
        i = (i + SIDE) % SIDE
        return xbuf.at[j, pl.ds(low, n), i] if ax == 0 else xbuf.at[j, i, pl.ds(low, n)]

    def first(ax, j, si):
        here = gblock(ax, j, mid(ax))
        return rcopy(
            here, here, gs.at[j, si], gr.at[j, si], (r, along(ax, x, z, 1 - 2 * si))
        )

    def first_on(ax, j, si):
        s = 1 - 2 * si
        ref = rows_of(gblock(ax, j, mid(ax) - s), si)
        return rcopy(ref, ref, gs.at[j, 2 + si], gr.at[j, 2 + si], (r, along(ax, x, z, s)))

    def second(ax, j, si):
        ref = ggroup(ax, j, end(ax), 0, SIDE)
        to = (r, along(1 - ax, x, z, 1 - 2 * si))
        return rcopy(ref, ref, gs.at[j, 4 + si], gr.at[j, 4 + si], to)

    def second_on(ax, j, si):
        s = 1 - 2 * si
        ref = ggroup(ax, j, end(ax) - s, 2 * si, 2)
        return rcopy(ref, ref, gs.at[j, 6 + si], gr.at[j, 6 + si], (r, along(1 - ax, x, z, s)))

    def ways(s, do):
        for si in (0, 1):
            both(s, lambda ax, j: do(ax, j, si))

    loop(0, ROWS_DEV, lambda b: load_cache(b).start())
    load_o.start()

    def stats_x(s):
        loop(0, 3, lambda d: stat_x(d).start())

    def stats_z(s):
        loop(0, 3, lambda d: stat_x(d).wait_recv())
        zmsg[0:16] = stx[0, 0:16] + stx[1, 0:16] + stx[2, 0:16] + stx[3, 0:16]
        for i in range(SIDE):
            zmsg[16 + 8 * i : 24 + 8 * i] = stx[i, 16:24]
        stz[z] = zmsg[...]
        loop(0, 3, lambda d: stat_z(d).start())

    def spread(i):
        rows = stz[i % SIDE, pl.ds(pl.multiple_of(16 + 8 * (i // SIDE), 8), 8)]
        gexp[i, 0:128] = jnp.broadcast_to(rows[0:1], (128, 128)).T
        gexp[i, 128:feats] = jnp.broadcast_to(rows[1:2], (128, 128)).T[0 : feats - 128]

    def stats_y(s):
        loop(0, 3, lambda d: stat_z(d).wait_recv())
        ymsg[...] = stz[0, 0:16] + stz[1, 0:16] + stz[2, 0:16] + stz[3, 0:16]
        sty[y] = ymsg[...]
        loop(0, 3, lambda d: stat_y(d).start())
        loop(0, N_COL, spread)

    def stats_core(s):
        loop(0, 3, lambda d: stat_y(d).wait_recv())
        cmsg[...] = sty[0] + sty[1] + sty[2] + sty[3]
        stc[core] = cmsg[...]
        stat_c.start()

    def stats_end(s):
        stat_c.wait_recv()
        total = stc[0] + stc[1]
        average = total[0:8] / n_features
        mi[0:8] = average
        mi[8:16] = lax.rsqrt(total[8:16] / n_features - average * average + EPSILON)
        load_q.wait()
        load_kv.wait()
        load_o.wait()

    def tokens_first(s):
        ways(s, lambda ax, j, si: first(ax, j, si).start())

    def tokens_first_on(s):
        def do(ax, j, si):
            first(ax, j, si).wait_recv()
            first_on(ax, j, si).start()

        ways(s, do)

    def tokens_second(s):
        ways(s, lambda ax, j, si: first_on(ax, j, si).wait_recv())
        ways(s, lambda ax, j, si: second(ax, j, si).start())

    def tokens_second_on(s):
        def do(ax, j, si):
            second(ax, j, si).wait_recv()
            second_on(ax, j, si).start()

        ways(s, do)

    def to_partner(s):
        return rcopy(pq.at[s, 1 - core], pqr.at[s], ps.at[s, 0], pr.at[s, 0], (partner, c))

    def project(s):
        ways(s, lambda ax, j, si: second_on(ax, j, si).wait_recv())
        for h in (0, 1):
            j = 2 * s + h
            mean, inverse = mi[pl.ds(j, 1), :], mi[pl.ds(8 + j, 1), :]
            for i in range(N_COL):
                t = xbuf[j, i // SIDE, i % SIDE].astype(F32)
                xn[feats * i : feats * (i + 1), LANES * h : LANES * (h + 1)] = (
                    (t - mean) * inverse * gexp[i]
                ).astype(BF16)
        partial = lax.dot_general(
            xn[...], qw[...], (((0,), (0,)), ((), ())), preferred_element_type=F32
        ).astype(BF16)
        for i in range(N_ROW):
            pq[s, i % 2, i // 2] = partial[block_rows * i : block_rows * (i + 1)]
        to_partner(s).start()

    def to_y(s, d):
        to = (r + 2 * d + 2) % N_ROW
        return rcopy(
            yq.at[s, to // 2], yqr.at[s, y], ps.at[s, 1 + d], pr.at[s, 1 + d], (to, c)
        )

    def sum_cores(s):
        to_partner(s).wait_recv()
        yq[s] = (pq[s, core].astype(F32) + pqr[s].astype(F32)).astype(BF16)
        loop(0, 3, lambda d: to_y(s, d).start())
        yqr[s, y] = yq[s, y]

    def scatter(src, dst, send_sem, recv_sem, s, d):
        to = (c + 1 + d) % N_COL
        return rcopy(src.at[s, to], dst.at[s, c], send_sem.at[s, d], recv_sem.at[s, d], (r, to))

    def rows_out(s):
        loop(0, 3, lambda d: to_y(s, d).wait_recv())
        total = yqr[s, 0].astype(F32)
        for i in range(1, SIDE):
            total = total + yqr[s, i].astype(F32)
        for b in (0, 1):
            for k in range(wide_parts):
                fold[:, b * wide_parts + k, :] = total[
                    N_COL * b : N_COL * (b + 1), LANES * k : LANES * (k + 1)
                ]
        slab[s] = fold[...]
        loop(0, N_COL - 1, lambda d: scatter(slab, slabr, as_, ar, s, d).start())
        slabr[s, c] = fold[c]

    scale = HD**-0.5

    def attend(s):
        loop(0, N_COL - 1, lambda d: scatter(slab, slabr, as_, ar, s, d).wait_recv())
        fold[...] = slabr[s]
        for b in (0, 1):
            position = lax.broadcasted_iota(jnp.int32, (1, kvc.shape[1]), 1)
            n = 2 * s + b
            load_cache(n).wait()
            for k in range(q_parts):
                qt[N_COL * (k // 2) : N_COL * (k // 2 + 1), LANES * (k % 2) : LANES * (k % 2 + 1)] = (
                    fold[:, b * wide_parts + k, :].astype(BF16)
                )
            for i in range(SIDE):
                kvf[n, 0:1, LANES * i : LANES * (i + 1)] = (
                    fold[SIDE * i, b * wide_parts + q_parts : b * wide_parts + q_parts + 1, :]
                    .astype(BF16)
                    .astype(F32)
                )
            fresh = kvf[n, 0:1, :]
            new_key, new_value = fresh[:, :HD], fresh[:, HD:]
            q = qt[...]
            scores = (
                lax.dot_general(
                    q, kvc[n, :, :HD], (((1,), (1,)), ((), ())), preferred_element_type=F32
                )
                * scale
            )
            scores = jnp.where(position < lengths[n], scores, NEGATIVE_FLOOR)
            new_score = jnp.sum(q.astype(F32) * new_key, axis=1, keepdims=True) * scale
            top = jnp.maximum(jnp.max(scores, axis=1, keepdims=True), new_score)
            weights = jnp.exp(scores - top)
            new_weight = jnp.exp(new_score - top)
            total = jnp.sum(weights, axis=1, keepdims=True) + new_weight
            context = jnp.dot(weights.astype(BF16), kvc[n, :, HD:], preferred_element_type=F32)
            context = context + new_weight.astype(BF16).astype(F32) * new_value
            context = context / total
            for k in range(q_parts):
                cfold[:, b * q_parts + k, :] = context[
                    N_COL * (k // 2) : N_COL * (k // 2 + 1), LANES * (k % 2) : LANES * (k % 2 + 1)
                ]
        cslab[s] = cfold[...]
        loop(0, N_COL - 1, lambda d: scatter(cslab, cslabr, cs, cr, s, d).start())
        cslabr[s, c] = cfold[c]

    def share(s, d):
        to = ((r + 2 * d + 2) % N_ROW, c)
        ref = allctx.at[s, r]
        return rcopy(ref, ref, os_.at[s, d], or_.at[s, d], to)

    def pass_on(s, d):
        ref = allctx.at[s, (r + 2 * (SIDE - 1 - d)) % N_ROW]
        return rcopy(ref, ref, os_.at[s, 3 + d], or_.at[s, 3 + d], (partner, c))

    def share_core(s):
        ref = allctx.at[s, r]
        return rcopy(ref, ref, os_.at[s, 6], or_.at[s, 6], (partner, c))

    def contexts_out(s):
        loop(0, N_COL - 1, lambda d: scatter(cslab, cslabr, cs, cr, s, d).wait_recv())
        cfold[...] = cslabr[s]
        for b in (0, 1):
            for k in range(q_parts):
                allctx[s, r, N_COL * b : N_COL * (b + 1), LANES * k : LANES * (k + 1)] = cfold[
                    :, b * q_parts + k, :
                ].astype(BF16)
        loop(0, 3, lambda d: share(s, d).start())
        share_core(s).start()

    def contexts_on(s):
        def do(d):
            share(s, d).wait_recv()
            pass_on(s, d).start()

        loop(0, 3, do)

    def group(ax, j, i, low, n):
        i = (i + SIDE) % SIDE
        return pbuf.at[j, i, pl.ds(low, n)] if ax == 0 else pbuf.at[j, pl.ds(low, n), i]

    def block(ax, j, i):
        i = (i + SIDE) % SIDE
        return pbuf.at[j, x, i] if ax == 0 else pbuf.at[j, i, z]

    def send_1a(ax, j, si):
        src = group(ax, j, mid(ax) + 2, 2 * si, 2)
        to = (r, along(ax, x, z, 1 - 2 * si))
        return rcopy(src, r1a.at[j, si], gs.at[j, 8 + si], gr.at[j, 8 + si], to)

    def send_1b(ax, j, si):
        s = 1 - 2 * si
        src = group(ax, j, mid(ax) + s, 0, SIDE)
        to = (r, along(ax, x, z, s))
        return rcopy(src, r1b.at[j, si], gs.at[j, 10 + si], gr.at[j, 10 + si], to)

    def send_2a(ax, j, si):
        src = rows_of(block(ax, j, end(ax) + 2), si)
        to = (r, along(1 - ax, x, z, 1 - 2 * si))
        return rcopy(src, rows_of(r2a.at[j], si), gs.at[j, 12 + si], gr.at[j, 12 + si], to)

    def send_2b(ax, j, si):
        s = 1 - 2 * si
        src = block(ax, j, end(ax) + s)
        to = (r, along(1 - ax, x, z, s))
        return rcopy(src, r2b.at[j, si], gs.at[j, 14 + si], gr.at[j, 14 + si], to)

    def project_out(s):
        share_core(s).wait_recv()
        loop(0, 3, lambda d: pass_on(s, d).wait_recv())

        def do(ax, j):
            context = allctx[s, 4 * ax : 4 * ax + 4].reshape(LANES, head_cols)
            term = jnp.dot(context, ow[...], preferred_element_type=F32)
            turned = term.astype(BF16).T
            for i in range(N_COL):
                pbuf[j, i // SIDE, i % SIDE] = turned[feats * i : feats * (i + 1)]
            for si in (0, 1):
                send_1a(ax, j, si).start()

        both(s, do)

    def sum_1b(s):
        def do(ax, j):
            for si in (0, 1):
                send_1a(ax, j, si).wait_recv()
                add_into(group(ax, j, mid(ax) + 1 - 2 * si, 2 * si, 2), r1a.at[j, si])
                send_1b(ax, j, si).start()

        both(s, do)

    def sum_2a(s):
        def do(ax, j):
            send_1b(ax, j, 0).wait_recv()
            send_1b(ax, j, 1).wait_recv()
            add_into(group(ax, j, mid(ax), 0, SIDE), r1b.at[j, 0], r1b.at[j, 1])
            for si in (0, 1):
                send_2a(ax, j, si).start()

        both(s, do)

    def sum_2b(s):
        def do(ax, j):
            for si in (0, 1):
                send_2a(ax, j, si).wait_recv()
                add_into(
                    rows_of(block(ax, j, end(ax) + 1 - 2 * si), si), rows_of(r2a.at[j], si)
                )
                send_2b(ax, j, si).start()

        both(s, do)

    def sum_end(s):
        def do(ax, j):
            send_2b(ax, j, 0).wait_recv()
            send_2b(ax, j, 1).wait_recv()
            total = (
                block(ax, j, end(ax))[...].astype(F32)
                + r2b[j, 0].astype(F32)
                + r2b[j, 1].astype(F32)
            )
            ot[j] = total.astype(BF16)

        both(s, do)

    steps = dict(
        st_x=stats_x,
        st_z=stats_z,
        st_y=stats_y,
        st_c=stats_core,
        st_end=stats_end,
        first=tokens_first,
        first_on=tokens_first_on,
        second=tokens_second,
        second_on=tokens_second_on,
        project=project,
        sum_cores=sum_cores,
        rows_out=rows_out,
        attend=attend,
        contexts_out=contexts_out,
        contexts_on=contexts_on,
        project_out=project_out,
        sum_1b=sum_1b,
        sum_2a=sum_2a,
        sum_2b=sum_2b,
        sum_end=sum_end,
    )
    names = list(steps)
    order = []
    for name, s in ORDER:
        order.append((names.index(name), s))
    def take(step, s, low, high):
        if high - low == 1:
            steps[names[low]](s)
            return
        middle = (low + high) // 2
        pl.when(step < middle)(lambda: take(step, s, low, middle))
        pl.when(step >= middle)(lambda: take(step, s, middle, high))

    def in_order(t):
        code = jnp.int32(0)
        for i, (step, s) in enumerate(order):
            code = jnp.where(t == i, step * QUARTERS + s, code)
        take(code // QUARTERS, code % QUARTERS, 0, len(names))

    loop(0, len(order), in_order)

    for h in (0, 1):
        total = jnp.zeros((feats, 4 * LANES), F32)
        for s in range(QUARTERS):
            total = total + lax.dot_general(
                ot[2 * s + h], perm[s], (((1,), (1,)), ((), ())), preferred_element_type=F32
            )
        out[:, 4 * LANES * h : 4 * LANES * (h + 1)] = total.astype(BF16)
    fresh = [kvf[n, 0:1, :] for n in range(ROWS_DEV)]
    kv_out[...] = jnp.concatenate(fresh, axis=0).astype(BF16)

    loop(0, 3, lambda d: stat_x(d).wait_send())
    loop(0, 3, lambda d: stat_z(d).wait_send())
    loop(0, 3, lambda d: stat_y(d).wait_send())
    stat_c.wait_send()

    def sent(s):
        for send in (first, first_on, second, second_on, send_1a, send_1b, send_2a, send_2b):
            ways(s, lambda ax, j, si: send(ax, j, si).wait_send())
        to_partner(s).wait_send()
        loop(0, 3, lambda d: to_y(s, d).wait_send())
        loop(0, N_COL - 1, lambda d: scatter(slab, slabr, as_, ar, s, d).wait_send())
        loop(0, N_COL - 1, lambda d: scatter(cslab, cslabr, cs, cr, s, d).wait_send())
        loop(0, 3, lambda d: share(s, d).wait_send())
        loop(0, 3, lambda d: pass_on(s, d).wait_send())
        share_core(s).wait_send()

    loop(0, QUARTERS, sent)


def shards(
    tokens, layer_norm_gain, query_weight, kv_weight, output_weight_matrix, kv_cache, lengths
):
    devices = lax.axis_size("row") * lax.axis_size("col")
    rows, feats = tokens.shape
    depth, head_cols = query_weight.shape
    heads = head_cols * N_COL // HD
    kv_cols = kv_weight.shape[1]
    wide = head_cols + LANES
    block_rows = LANES // 4
    vmem = pl.BlockSpec(memory_space=pltpu.VMEM)
    smem = pl.BlockSpec(memory_space=pltpu.SMEM)
    anywhere = pl.BlockSpec(memory_space=pl.ANY)
    dma = pltpu.SemaphoreType.DMA
    slabs = pltpu.VMEM((QUARTERS, N_COL, 16, LANES), F32)
    branch, new_kv = pl.pallas_call(
        functools.partial(kernel, feats * devices),
        out_shape=(
            jax.ShapeDtypeStruct((feats, rows), BF16),
            jax.ShapeDtypeStruct((ROWS_DEV, kv_cols), BF16),
        ),
        in_specs=[vmem, vmem, anywhere, anywhere, anywhere, anywhere, smem],
        out_specs=(vmem, vmem),
        scratch_shapes=[
            pltpu.VMEM((QUARTERS, 4 * LANES, LANES), BF16),
            pltpu.VMEM((CHUNKS, SIDE, SIDE, feats, LANES), BF16),
            pltpu.VMEM((depth, wide), BF16),
            pltpu.VMEM(output_weight_matrix.shape, BF16),
            pltpu.VMEM(kv_cache.shape, BF16),
            pltpu.VMEM((N_COL, feats, LANES), F32),
            pltpu.VMEM((depth, 2 * LANES), BF16),
            pltpu.VMEM((QUARTERS, 2, SIDE, block_rows, wide), BF16),
            pltpu.VMEM((QUARTERS, SIDE, block_rows, wide), BF16),
            pltpu.VMEM((QUARTERS, SIDE, block_rows, wide), BF16),
            pltpu.VMEM((QUARTERS, SIDE, block_rows, wide), BF16),
            slabs,
            slabs,
            slabs,
            slabs,
            pltpu.VMEM((N_COL, 16, LANES), F32),
            pltpu.VMEM((N_COL, 16, LANES), F32),
            pltpu.VMEM((heads, HD), BF16),
            pltpu.VMEM((ROWS_DEV, 8, kv_cols), F32),
            pltpu.VMEM((QUARTERS, N_ROW, block_rows, head_cols), BF16),
            pltpu.VMEM((CHUNKS, SIDE, SIDE, feats, LANES), BF16),
            pltpu.VMEM((CHUNKS, 2, 2, feats, LANES), BF16),
            pltpu.VMEM((CHUNKS, 2, SIDE, feats, LANES), BF16),
            pltpu.VMEM((CHUNKS, feats, LANES), BF16),
            pltpu.VMEM((CHUNKS, 2, feats, LANES), BF16),
            pltpu.VMEM((CHUNKS, feats, LANES), BF16),
            pltpu.VMEM((SIDE, 24, LANES), F32),
            pltpu.VMEM((SIDE, 48, LANES), F32),
            pltpu.VMEM((SIDE, 16, LANES), F32),
            pltpu.VMEM((2, 16, LANES), F32),
            pltpu.VMEM((24, LANES), F32),
            pltpu.VMEM((48, LANES), F32),
            pltpu.VMEM((16, LANES), F32),
            pltpu.VMEM((16, LANES), F32),
            pltpu.VMEM((16, LANES), F32),
            dma((3,)),
            dma((ROWS_DEV,)),
            dma((CHUNKS, 16)),
            dma((CHUNKS, 16)),
            dma((QUARTERS, 7)),
            dma((QUARTERS, 7)),
            dma((QUARTERS, 4)),
            dma((QUARTERS, 4)),
            dma((QUARTERS, N_COL - 1)),
            dma((QUARTERS, N_COL - 1)),
            dma((QUARTERS, N_COL - 1)),
            dma((QUARTERS, N_COL - 1)),
            dma((10,)),
            dma((10,)),
        ],
        compiler_params=pltpu.CompilerParams(
            collective_id=0, has_side_effects=True, vmem_limit_bytes=VMEM_BYTES
        ),
        name="decode",
    )(
        tokens.T,
        layer_norm_gain.reshape(1, feats),
        query_weight,
        kv_weight,
        output_weight_matrix,
        kv_cache,
        lengths,
    )
    return branch.T, new_kv


def solution(mesh):
    placed = (
        P(None, ("row", "col")),
        P(("row", "col")),
        P("row", "col"),
        P("row", None),
        P("col", "row"),
        P(("row", "col"), None, None),
        P(("row", "col")),
    )
    return jax.shard_map(
        shards,
        mesh=mesh,
        in_specs=placed,
        out_specs=(P(None, ("row", "col")), P(("row", "col"), None)),
        check_vma=False,
    )
```

time: 515 us -> 106 us (0.21)
  waiting for transfers between devices: 219 us -> 0 us
  Pallas kernels: 0 us -> 98.8 us
  blocking collectives: 81.9 us -> 0 us
  other arithmetic: 80 us -> 0 us
  local copies, waits for them, and re-layouts: 60 us -> 4.21 us
  matrix products: 51 us -> 0 us
  between operations: 13.8 us -> 0.64 us
  starting transfers between devices: 5.69 us -> 0 us
    reduce_scatter x3 -> x0, waiting for transfers between devices: 113 us -> none  [the longest x1 80.3 us: shards(): lax.psum_scatter(out_term.astype(jnp.bfloat16), 'col', scatter_dimension=...]
    pallas_call x0 -> x1, Pallas kernels: none -> 98.8 us  [shards(): pl.pallas_call(functools.partial(kernel, feats * devices), out_shape=(jax...]
    all_gather x2 -> x0, waiting for transfers between devices: 73.7 us -> none  [the longest x1 51.8 us: shards(): portion = lax.all_gather(normed, 'col', axis=1, tiled=True)]
    unnamed x1 -> x0, other arithmetic: 68.7 us -> none
    psum x1 -> x0, blocking collectives: 66.7 us -> none  [shards(): lax.psum((jnp.sum(floats, axis=1), jnp.sum(floats * floats, axis=1)), ('r...]
    dot_general x16 -> x0, matrix products: 51 us -> none  [the longest x8 22.2 us: block_scores(): jnp.einsum('mqg,mfg->mqf', queries, kv_block[:, :, :head_dim], preferred_...]
    all_to_all x1 -> x0, waiting for transfers between devices: 32.6 us -> none  [shards(): lax.all_to_all(query_four, 'col', split_axis=1, concat_axis=3, tiled=True)]
    unnamed x12 -> x2, local copies, waits for them, and re-layouts: 20 us -> 2.99 us
  transfers between devices with their start and end apart: 6 -> 0, of which waited for: 5 -> 0; matrix products, arithmetic and copies ran while one was open for 3% -> 0% of each run, Pallas kernels for 0% -> 0%
where the time goes in v2:
time: 106 us; the launch traced here: 104 us
  Pallas kernels  98.8 us (93%)
  local copies, waits for them, and re-layouts  4.21 us (4%)
    pallas_call x1, Pallas kernels, shards(): pl.pallas_call(functools.partial(kernel, feats * devices), out_shape=(jax...  98.8 us
    unnamed x2, local copies, waits for them, and re-layouts  2.99 us

profile of v2, /device:TPU:8, one launch (start us, length us, event | category | flops | bytes accessed | tf_op | source)
XLA Modules:
  0.0 103.6 jit_solution(321210867092170392)
XLA Ops:
  0.6 1.2 %reshape.7.gain = bf16[1,144]{1,0:T(2,128)(2,1)} reshape(bf16[144]{0:T(256)(128)(2,1)} %param.8) | data formatting | bytes 576 | tf_op jit(solution)/shard_map/reshape | solution.py:694
  1.9 98.8 %decode.1 = (bf16[144,1024]{1,0:T(8,128)(2,1)}, bf16[8,512]{1,0:T(8,128)(2,1)}) custom-call(bf16[144,1024]{1,0:T(8,128)(2,1)} %bitcast.3, bf16[1,144]{1,0:T(2,128)(2,1)} %reshape.7.gain, bf16[2304,768]{1,0:T(8,128)(2,1)} %wq.1, bf16[2304,512]{1,0:T(8,128)(2,1)} %wkv.1, bf16[768,2304]{1,0:T(8,128)(2,1)} %wo.1, bf16[8,2048,512]{2,1,0:T(8,128)(2,1)} %cache.1, ...), custom_call_target="tpu_custom_call" | custom-call | tf_op jit(solution)/shard_map/decode/pallas_call | solution.py:629
  100.6 1.7 %copy.11 = bf16[1024,144]{0,1:T(8,128)(2,1)} copy(bf16[1024,144]{0,1:T(8,128)(2,1)} %bitcast.2) | data formatting | bytes 589824
  102.3 1.3 %copy.12 = bf16[8,512]{1,0:T(8,128)(2,1)} copy(bf16[8,512]{1,0:T(8,128)(2,1)} %get-tuple-element.9) | data formatting | bytes 16384

commit v3 on v2

--- a/solution.py
+++ b/solution.py
@@ -20,17 +20,17 @@
 CHUNKS = 2 * QUARTERS
 HALF = 80
 ORDER = [
-    ("first", 2), ("first", 1), ("first", 3), ("st_x", 0), ("first", 0), ("first_on", 2),
-    ("first_on", 1), ("first_on", 3), ("st_z", 0), ("second", 2), ("second", 1), ("first_on", 0),
-    ("st_y", 0), ("st_c", 0), ("second_on", 2), ("second_on", 1), ("second", 0), ("second", 3),
-    ("st_end", 0), ("project", 2), ("sum_cores", 2), ("project", 1), ("sum_cores", 1), ("second_on", 0),
-    ("rows_out", 2), ("second_on", 3), ("project", 0), ("rows_out", 1), ("sum_cores", 0), ("project", 3),
-    ("attend", 2), ("sum_cores", 3), ("rows_out", 0), ("attend", 1), ("contexts_out", 2), ("rows_out", 3),
-    ("attend", 0), ("contexts_out", 1), ("contexts_on", 2), ("project_out", 2), ("attend", 3), ("contexts_out", 0),
-    ("contexts_on", 1), ("project_out", 1), ("sum_1b", 2), ("contexts_out", 3), ("contexts_on", 0), ("project_out", 0),
-    ("sum_1b", 1), ("contexts_on", 3), ("sum_2a", 2), ("project_out", 3), ("sum_1b", 0), ("sum_1b", 3),
-    ("sum_2a", 1), ("sum_2b", 2), ("sum_2a", 0), ("sum_2a", 3), ("sum_2b", 1), ("sum_end", 2),
-    ("sum_2b", 0), ("sum_2b", 3), ("sum_end", 1), ("sum_end", 0), ("sum_end", 3),
+    ("first", 3), ("first", 1), ("first", 0), ("first", 2), ("st_x", 0), ("first_on", 3),
+    ("first_on", 0), ("first_on", 1), ("first_on", 2), ("st_z", 0), ("second", 3), ("second", 1),
+    ("st_y", 0), ("second_on", 3), ("second", 0), ("second_on", 1), ("st_c", 0), ("second", 2),
+    ("st_end", 0), ("project", 3), ("sum_cores", 3), ("second_on", 0), ("project", 1), ("sum_cores", 1),
+    ("rows_out", 3), ("second_on", 2), ("project", 0), ("sum_cores", 0), ("rows_out", 1), ("project", 2),
+    ("attend", 3), ("sum_cores", 2), ("rows_out", 0), ("attend", 1), ("contexts_out", 3), ("rows_out", 2),
+    ("attend", 0), ("contexts_out", 1), ("contexts_on", 3), ("project_out", 3), ("attend", 2), ("contexts_out", 0),
+    ("contexts_on", 1), ("project_out", 1), ("sum_1b", 3), ("contexts_out", 2), ("contexts_on", 0), ("project_out", 0),
+    ("sum_1b", 1), ("contexts_on", 2), ("project_out", 2), ("sum_1b", 0), ("sum_1b", 2), ("sum_2a", 1),
+    ("sum_2a", 0), ("sum_2a", 3), ("sum_2a", 2), ("sum_2b", 1), ("sum_2b", 0), ("sum_2b", 3),
+    ("sum_2b", 2), ("sum_end", 1), ("sum_end", 3), ("sum_end", 0), ("sum_end", 2),
 ]
 VMEM_BYTES = 60 * 1024 * 1024
 F32, BF16 = jnp.float32, jnp.bfloat16
@@ -61,6 +61,10 @@
     lax.fori_loop(low, high, step, 0)
 
 
+def landed(ref, sem):
+    pltpu.make_async_copy(ref, ref, sem).wait()
+
+
 def greet(peers):
     barrier = pltpu.get_barrier_semaphore()
     count = 0
@@ -71,7 +75,7 @@
 
         loop(0, number, hello)
         count += number
-    pl.semaphore_wait(barrier, count)
+    return count
 
 
 def rows_of(ref, si):
@@ -163,6 +167,14 @@
     wide = wide_parts * LANES
     block_rows = LANES // 4
 
+    peers = greet(
+        [
+            (N_COL - 1, lambda d: (r, (c + 1 + d) % N_COL)),
+            (1, lambda d: (partner, c)),
+            (3, lambda d: ((r + 2 * d + 2) % N_ROW, c)),
+        ]
+    )
+
     load_q = pltpu.make_async_copy(wq, qw.at[:, pl.ds(0, head_cols)], w_sem.at[0])
     load_kv = pltpu.make_async_copy(
         wkv.at[:, pl.ds(pl.multiple_of(x * LANES, LANES), LANES)],
@@ -175,6 +187,9 @@
 
     def load_cache(b):
         return pltpu.make_async_copy(cache.at[b], kvc.at[b], k_sem.at[b])
+
+    loop(0, ROWS_DEV, lambda b: load_cache(b).start())
+    load_o.start()
 
     row = lax.broadcasted_iota(jnp.int32, (4 * LANES, LANES), 0)
     lane = lax.broadcasted_iota(jnp.int32, (4 * LANES, LANES), 1)
@@ -197,7 +212,7 @@
         squares.append(jnp.sum(t * t, axis=0, keepdims=True))
     smsg[0:8] = jnp.concatenate(sums, axis=0)
     smsg[8:16] = jnp.concatenate(squares, axis=0)
-    gains = gain[...].astype(F32)
+    gains = gain[...].astype(F32).reshape(1, feats)
     smsg[16:24] = jnp.zeros((8, LANES), F32)
     smsg[16:17] = gains[:, 0:LANES]
     smsg[17:18, 0 : feats - LANES] = gains[:, LANES:feats]
@@ -205,24 +220,18 @@
 
     fold[...] = jnp.zeros_like(fold)
     cfold[...] = jnp.zeros_like(cfold)
-    greet(
-        [
-            (N_COL - 1, lambda d: (r, (c + 1 + d) % N_COL)),
-            (1, lambda d: (partner, c)),
-            (3, lambda d: ((r + 2 * d + 2) % N_ROW, c)),
-        ]
-    )
+    pl.semaphore_wait(pltpu.get_barrier_semaphore(), peers)
 
     def stat_x(d):
-        return rcopy(smsg, stx.at[x], ss.at[d], sr.at[d], (r, along(0, x, z, d + 1)))
+        return rcopy(smsg, stx.at[x], ss.at[0], sr.at[0], (r, along(0, x, z, d + 1)))
 
     def stat_z(d):
-        return rcopy(zmsg, stz.at[z], ss.at[3 + d], sr.at[3 + d], (r, along(1, x, z, d + 1)))
+        return rcopy(zmsg, stz.at[z], ss.at[1], sr.at[1], (r, along(1, x, z, d + 1)))
 
     def stat_y(d):
-        return rcopy(ymsg, sty.at[y], ss.at[6 + d], sr.at[6 + d], ((r + 2 * d + 2) % N_ROW, c))
-
-    stat_c = rcopy(cmsg, stc.at[core], ss.at[9], sr.at[9], (partner, c))
+        return rcopy(ymsg, sty.at[y], ss.at[2], sr.at[2], ((r + 2 * d + 2) % N_ROW, c))
+
+    stat_c = rcopy(cmsg, stc.at[core], ss.at[3], sr.at[3], (partner, c))
 
     def mid(ax):
         return x if ax == 0 else z
@@ -241,36 +250,33 @@
     def first(ax, j, si):
         here = gblock(ax, j, mid(ax))
         return rcopy(
-            here, here, gs.at[j, si], gr.at[j, si], (r, along(ax, x, z, 1 - 2 * si))
+            here, here, gs.at[j // 2, 0], gr.at[j // 2, 0], (r, along(ax, x, z, 1 - 2 * si))
         )
 
     def first_on(ax, j, si):
         s = 1 - 2 * si
         ref = rows_of(gblock(ax, j, mid(ax) - s), si)
-        return rcopy(ref, ref, gs.at[j, 2 + si], gr.at[j, 2 + si], (r, along(ax, x, z, s)))
+        return rcopy(ref, ref, gs.at[j // 2, 1], gr.at[j // 2, 1], (r, along(ax, x, z, s)))
 
     def second(ax, j, si):
         ref = ggroup(ax, j, end(ax), 0, SIDE)
         to = (r, along(1 - ax, x, z, 1 - 2 * si))
-        return rcopy(ref, ref, gs.at[j, 4 + si], gr.at[j, 4 + si], to)
+        return rcopy(ref, ref, gs.at[j // 2, 2], gr.at[j // 2, 2], to)
 
     def second_on(ax, j, si):
         s = 1 - 2 * si
         ref = ggroup(ax, j, end(ax) - s, 2 * si, 2)
-        return rcopy(ref, ref, gs.at[j, 6 + si], gr.at[j, 6 + si], (r, along(1 - ax, x, z, s)))
+        return rcopy(ref, ref, gs.at[j // 2, 3], gr.at[j // 2, 3], (r, along(1 - ax, x, z, s)))
 
     def ways(s, do):
         for si in (0, 1):
             both(s, lambda ax, j: do(ax, j, si))
 
-    loop(0, ROWS_DEV, lambda b: load_cache(b).start())
-    load_o.start()
-
     def stats_x(s):
         loop(0, 3, lambda d: stat_x(d).start())
 
     def stats_z(s):
-        loop(0, 3, lambda d: stat_x(d).wait_recv())
+        landed(stx.at[pl.ds(0, 3)], sr.at[0])
         zmsg[0:16] = stx[0, 0:16] + stx[1, 0:16] + stx[2, 0:16] + stx[3, 0:16]
         for i in range(SIDE):
             zmsg[16 + 8 * i : 24 + 8 * i] = stx[i, 16:24]
@@ -283,14 +289,14 @@
         gexp[i, 128:feats] = jnp.broadcast_to(rows[1:2], (128, 128)).T[0 : feats - 128]
 
     def stats_y(s):
-        loop(0, 3, lambda d: stat_z(d).wait_recv())
+        landed(stz.at[pl.ds(0, 3)], sr.at[1])
         ymsg[...] = stz[0, 0:16] + stz[1, 0:16] + stz[2, 0:16] + stz[3, 0:16]
         sty[y] = ymsg[...]
         loop(0, 3, lambda d: stat_y(d).start())
         loop(0, N_COL, spread)
 
     def stats_core(s):
-        loop(0, 3, lambda d: stat_y(d).wait_recv())
+        landed(sty.at[pl.ds(0, 3)], sr.at[2])
         cmsg[...] = sty[0] + sty[1] + sty[2] + sty[3]
         stc[core] = cmsg[...]
         stat_c.start()
@@ -309,28 +315,22 @@
         ways(s, lambda ax, j, si: first(ax, j, si).start())
 
     def tokens_first_on(s):
-        def do(ax, j, si):
-            first(ax, j, si).wait_recv()
-            first_on(ax, j, si).start()
-
-        ways(s, do)
+        landed(xbuf.at[2 * s, 0], gr.at[s, 0])
+        ways(s, lambda ax, j, si: first_on(ax, j, si).start())
 
     def tokens_second(s):
-        ways(s, lambda ax, j, si: first_on(ax, j, si).wait_recv())
+        landed(xbuf.at[2 * s, 0, pl.ds(0, 2)], gr.at[s, 1])
         ways(s, lambda ax, j, si: second(ax, j, si).start())
 
     def tokens_second_on(s):
-        def do(ax, j, si):
-            second(ax, j, si).wait_recv()
-            second_on(ax, j, si).start()
-
-        ways(s, do)
+        landed(xbuf.at[2 * s], gr.at[s, 2])
+        ways(s, lambda ax, j, si: second_on(ax, j, si).start())
 
     def to_partner(s):
         return rcopy(pq.at[s, 1 - core], pqr.at[s], ps.at[s, 0], pr.at[s, 0], (partner, c))
 
     def project(s):
-        ways(s, lambda ax, j, si: second_on(ax, j, si).wait_recv())
+        landed(xbuf.at[2 * s, pl.ds(0, 2)], gr.at[s, 3])
         for h in (0, 1):
             j = 2 * s + h
             mean, inverse = mi[pl.ds(j, 1), :], mi[pl.ds(8 + j, 1), :]
@@ -349,7 +349,7 @@
     def to_y(s, d):
         to = (r + 2 * d + 2) % N_ROW
         return rcopy(
-            yq.at[s, to // 2], yqr.at[s, y], ps.at[s, 1 + d], pr.at[s, 1 + d], (to, c)
+            yq.at[s, to // 2], yqr.at[s, y], ps.at[s, 1], pr.at[s, 1], (to, c)
         )
 
     def sum_cores(s):
@@ -360,10 +360,10 @@
 
     def scatter(src, dst, send_sem, recv_sem, s, d):
         to = (c + 1 + d) % N_COL
-        return rcopy(src.at[s, to], dst.at[s, c], send_sem.at[s, d], recv_sem.at[s, d], (r, to))
+        return rcopy(src.at[s, to], dst.at[s, c], send_sem.at[s], recv_sem.at[s], (r, to))
 
     def rows_out(s):
-        loop(0, 3, lambda d: to_y(s, d).wait_recv())
+        landed(yqr.at[s, pl.ds(0, 3)], pr.at[s, 1])
         total = yqr[s, 0].astype(F32)
         for i in range(1, SIDE):
             total = total + yqr[s, i].astype(F32)
@@ -372,32 +372,30 @@
                 fold[:, b * wide_parts + k, :] = total[
                     N_COL * b : N_COL * (b + 1), LANES * k : LANES * (k + 1)
                 ]
-        slab[s] = fold[...]
+        slab[s] = fold[...].astype(BF16)
         loop(0, N_COL - 1, lambda d: scatter(slab, slabr, as_, ar, s, d).start())
-        slabr[s, c] = fold[c]
+        slabr[s, c] = slab[s, c]
 
     scale = HD**-0.5
 
     def attend(s):
-        loop(0, N_COL - 1, lambda d: scatter(slab, slabr, as_, ar, s, d).wait_recv())
-        fold[...] = slabr[s]
+        landed(slabr.at[s, pl.ds(0, N_COL - 1)], ar.at[s])
+        fold[...] = slabr[s].astype(F32)
+        position = lax.broadcasted_iota(jnp.int32, (1, kvc.shape[1]), 1)
+        rows = []
         for b in (0, 1):
-            position = lax.broadcasted_iota(jnp.int32, (1, kvc.shape[1]), 1)
+            for k in range(q_parts):
+                at = slice(N_COL * (k // 2), N_COL * (k // 2 + 1))
+                qt[b, at, LANES * (k % 2) : LANES * (k % 2 + 1)] = fold[
+                    :, b * wide_parts + k, :
+                ].astype(BF16)
+            for i in range(SIDE):
+                k = b * wide_parts + q_parts
+                kvf[2 * s + b, 0:1, LANES * i : LANES * (i + 1)] = fold[SIDE * i, k : k + 1, :]
+        for b in (0, 1):
             n = 2 * s + b
             load_cache(n).wait()
-            for k in range(q_parts):
-                qt[N_COL * (k // 2) : N_COL * (k // 2 + 1), LANES * (k % 2) : LANES * (k % 2 + 1)] = (
-                    fold[:, b * wide_parts + k, :].astype(BF16)
-                )
-            for i in range(SIDE):
-                kvf[n, 0:1, LANES * i : LANES * (i + 1)] = (
-                    fold[SIDE * i, b * wide_parts + q_parts : b * wide_parts + q_parts + 1, :]
-                    .astype(BF16)
-                    .astype(F32)
-                )
-            fresh = kvf[n, 0:1, :]
-            new_key, new_value = fresh[:, :HD], fresh[:, HD:]
-            q = qt[...]
+            q, new_key = qt[b], kvf[n, 0:1, :HD]
             scores = (
                 lax.dot_general(
                     q, kvc[n, :, :HD], (((1,), (1,)), ((), ())), preferred_element_type=F32
@@ -406,37 +404,43 @@
             )
             scores = jnp.where(position < lengths[n], scores, NEGATIVE_FLOOR)
             new_score = jnp.sum(q.astype(F32) * new_key, axis=1, keepdims=True) * scale
+            rows.append((n, scores, new_score))
+        weighed = []
+        for n, scores, new_score in rows:
             top = jnp.maximum(jnp.max(scores, axis=1, keepdims=True), new_score)
             weights = jnp.exp(scores - top)
             new_weight = jnp.exp(new_score - top)
             total = jnp.sum(weights, axis=1, keepdims=True) + new_weight
-            context = jnp.dot(weights.astype(BF16), kvc[n, :, HD:], preferred_element_type=F32)
+            weighed.append((n, weights.astype(BF16), new_weight, total))
+        for b, (n, weights, new_weight, total) in enumerate(weighed):
+            new_value = kvf[n, 0:1, HD:]
+            context = jnp.dot(weights, kvc[n, :, HD:], preferred_element_type=F32)
             context = context + new_weight.astype(BF16).astype(F32) * new_value
             context = context / total
             for k in range(q_parts):
                 cfold[:, b * q_parts + k, :] = context[
                     N_COL * (k // 2) : N_COL * (k // 2 + 1), LANES * (k % 2) : LANES * (k % 2 + 1)
                 ]
-        cslab[s] = cfold[...]
+        cslab[s] = cfold[...].astype(BF16)
         loop(0, N_COL - 1, lambda d: scatter(cslab, cslabr, cs, cr, s, d).start())
-        cslabr[s, c] = cfold[c]
+        cslabr[s, c] = cslab[s, c]
 
     def share(s, d):
         to = ((r + 2 * d + 2) % N_ROW, c)
         ref = allctx.at[s, r]
-        return rcopy(ref, ref, os_.at[s, d], or_.at[s, d], to)
+        return rcopy(ref, ref, os_.at[s], or_.at[s, d], to)
 
     def pass_on(s, d):
         ref = allctx.at[s, (r + 2 * (SIDE - 1 - d)) % N_ROW]
-        return rcopy(ref, ref, os_.at[s, 3 + d], or_.at[s, 3 + d], (partner, c))
+        return rcopy(ref, ref, os_.at[s], or_.at[s, 3], (partner, c))
 
     def share_core(s):
         ref = allctx.at[s, r]
-        return rcopy(ref, ref, os_.at[s, 6], or_.at[s, 6], (partner, c))
+        return rcopy(ref, ref, os_.at[s], or_.at[s, 3], (partner, c))
 
     def contexts_out(s):
-        loop(0, N_COL - 1, lambda d: scatter(cslab, cslabr, cs, cr, s, d).wait_recv())
-        cfold[...] = cslabr[s]
+        landed(cslabr.at[s, pl.ds(0, N_COL - 1)], cr.at[s])
+        cfold[...] = cslabr[s].astype(F32)
         for b in (0, 1):
             for k in range(q_parts):
                 allctx[s, r, N_COL * b : N_COL * (b + 1), LANES * k : LANES * (k + 1)] = cfold[
@@ -463,28 +467,27 @@
     def send_1a(ax, j, si):
         src = group(ax, j, mid(ax) + 2, 2 * si, 2)
         to = (r, along(ax, x, z, 1 - 2 * si))
-        return rcopy(src, r1a.at[j, si], gs.at[j, 8 + si], gr.at[j, 8 + si], to)
+        return rcopy(src, r1a.at[j, si], gs.at[j // 2, 4], gr.at[j // 2, 4], to)
 
     def send_1b(ax, j, si):
         s = 1 - 2 * si
         src = group(ax, j, mid(ax) + s, 0, SIDE)
         to = (r, along(ax, x, z, s))
-        return rcopy(src, r1b.at[j, si], gs.at[j, 10 + si], gr.at[j, 10 + si], to)
+        return rcopy(src, r1b.at[j, si], gs.at[j // 2, 5], gr.at[j // 2, 5], to)
 
     def send_2a(ax, j, si):
         src = rows_of(block(ax, j, end(ax) + 2), si)
         to = (r, along(1 - ax, x, z, 1 - 2 * si))
-        return rcopy(src, rows_of(r2a.at[j], si), gs.at[j, 12 + si], gr.at[j, 12 + si], to)
+        return rcopy(src, rows_of(r2a.at[j], si), gs.at[j // 2, 6], gr.at[j // 2, 6], to)
 
     def send_2b(ax, j, si):
         s = 1 - 2 * si
         src = block(ax, j, end(ax) + s)
         to = (r, along(1 - ax, x, z, s))
-        return rcopy(src, r2b.at[j, si], gs.at[j, 14 + si], gr.at[j, 14 + si], to)
+        return rcopy(src, r2b.at[j, si], gs.at[j // 2, 7], gr.at[j // 2, 7], to)
 
     def project_out(s):
-        share_core(s).wait_recv()
-        loop(0, 3, lambda d: pass_on(s, d).wait_recv())
+        landed(allctx.at[s, pl.ds(0, 4)], or_.at[s, 3])
 
         def do(ax, j):
             context = allctx[s, 4 * ax : 4 * ax + 4].reshape(LANES, head_cols)
@@ -498,18 +501,19 @@
         both(s, do)
 
     def sum_1b(s):
+        landed(pbuf.at[2 * s, pl.ds(0, 2)], gr.at[s, 4])
+
         def do(ax, j):
             for si in (0, 1):
-                send_1a(ax, j, si).wait_recv()
                 add_into(group(ax, j, mid(ax) + 1 - 2 * si, 2 * si, 2), r1a.at[j, si])
                 send_1b(ax, j, si).start()
 
         both(s, do)
 
     def sum_2a(s):
+        landed(pbuf.at[2 * s], gr.at[s, 5])
+
         def do(ax, j):
-            send_1b(ax, j, 0).wait_recv()
-            send_1b(ax, j, 1).wait_recv()
             add_into(group(ax, j, mid(ax), 0, SIDE), r1b.at[j, 0], r1b.at[j, 1])
             for si in (0, 1):
                 send_2a(ax, j, si).start()
@@ -517,9 +521,10 @@
         both(s, do)
 
     def sum_2b(s):
+        landed(pbuf.at[2 * s, 0, pl.ds(0, 2)], gr.at[s, 6])
+
         def do(ax, j):
             for si in (0, 1):
-                send_2a(ax, j, si).wait_recv()
                 add_into(
                     rows_of(block(ax, j, end(ax) + 1 - 2 * si), si), rows_of(r2a.at[j], si)
                 )
@@ -528,9 +533,9 @@
         both(s, do)
 
     def sum_end(s):
+        landed(pbuf.at[2 * s, 0], gr.at[s, 7])
+
         def do(ax, j):
-            send_2b(ax, j, 0).wait_recv()
-            send_2b(ax, j, 1).wait_recv()
             total = (
                 block(ax, j, end(ax))[...].astype(F32)
                 + r2b[j, 0].astype(F32)
@@ -592,23 +597,45 @@
     fresh = [kvf[n, 0:1, :] for n in range(ROWS_DEV)]
     kv_out[...] = jnp.concatenate(fresh, axis=0).astype(BF16)
 
-    loop(0, 3, lambda d: stat_x(d).wait_send())
-    loop(0, 3, lambda d: stat_z(d).wait_send())
-    loop(0, 3, lambda d: stat_y(d).wait_send())
+    landed(stx.at[pl.ds(0, 3)], ss.at[0])
+    landed(stz.at[pl.ds(0, 3)], ss.at[1])
+    landed(sty.at[pl.ds(0, 3)], ss.at[2])
     stat_c.wait_send()
 
     def sent(s):
-        for send in (first, first_on, second, second_on, send_1a, send_1b, send_2a, send_2b):
-            ways(s, lambda ax, j, si: send(ax, j, si).wait_send())
+        for k, buf in ((0, xbuf), (4, pbuf)):
+            both_ways = (buf.at[2 * s, pl.ds(0, 2)], buf.at[2 * s])
+            part, whole = buf.at[2 * s, 0, pl.ds(0, 2)], buf.at[2 * s, 0]
+            sizes = (whole, part, both_ways[1], both_ways[0])
+            sizes = sizes if k == 0 else (both_ways[0], both_ways[1], part, whole)
+            for i, ref in enumerate(sizes):
+                landed(ref, gs.at[s, k + i])
         to_partner(s).wait_send()
-        loop(0, 3, lambda d: to_y(s, d).wait_send())
-        loop(0, N_COL - 1, lambda d: scatter(slab, slabr, as_, ar, s, d).wait_send())
-        loop(0, N_COL - 1, lambda d: scatter(cslab, cslabr, cs, cr, s, d).wait_send())
-        loop(0, 3, lambda d: share(s, d).wait_send())
-        loop(0, 3, lambda d: pass_on(s, d).wait_send())
-        share_core(s).wait_send()
+        landed(yqr.at[s, pl.ds(0, 3)], ps.at[s, 1])
+        landed(slab.at[s, pl.ds(0, N_COL - 1)], as_.at[s])
+        landed(cslab.at[s, pl.ds(0, N_COL - 1)], cs.at[s])
+        landed(allctx.at[s, pl.ds(0, 7)], os_.at[s])
 
     loop(0, QUARTERS, sent)
+
+
+def hand_over_kernel(branch, new_kv, branch_out, new_kv_out):
+    branch_out[...] = branch[...]
+    new_kv_out[...] = new_kv[...]
+
+
+def hand_over(branch, new_kv):
+    vmem = pl.BlockSpec(memory_space=pltpu.VMEM)
+    return pl.pallas_call(
+        hand_over_kernel,
+        out_shape=(
+            jax.ShapeDtypeStruct(branch.shape, branch.dtype),
+            jax.ShapeDtypeStruct(new_kv.shape, new_kv.dtype),
+        ),
+        in_specs=[vmem, vmem],
+        out_specs=(vmem, vmem),
+        name="hand_over",
+    )(branch, new_kv)
 
 
 def shards(
@@ -625,7 +652,7 @@
     smem = pl.BlockSpec(memory_space=pltpu.SMEM)
     anywhere = pl.BlockSpec(memory_space=pl.ANY)
     dma = pltpu.SemaphoreType.DMA
-    slabs = pltpu.VMEM((QUARTERS, N_COL, 16, LANES), F32)
+    slabs = pltpu.VMEM((QUARTERS, N_COL, 16, LANES), BF16)
     branch, new_kv = pl.pallas_call(
         functools.partial(kernel, feats * devices),
         out_shape=(
@@ -652,7 +679,7 @@
             slabs,
             pltpu.VMEM((N_COL, 16, LANES), F32),
             pltpu.VMEM((N_COL, 16, LANES), F32),
-            pltpu.VMEM((heads, HD), BF16),
+            pltpu.VMEM((2, heads, HD), BF16),
             pltpu.VMEM((ROWS_DEV, 8, kv_cols), F32),
             pltpu.VMEM((QUARTERS, N_ROW, block_rows, head_cols), BF16),
             pltpu.VMEM((CHUNKS, SIDE, SIDE, feats, LANES), BF16),
@@ -672,18 +699,18 @@
             pltpu.VMEM((16, LANES), F32),
             dma((3,)),
             dma((ROWS_DEV,)),
-            dma((CHUNKS, 16)),
-            dma((CHUNKS, 16)),
-            dma((QUARTERS, 7)),
-            dma((QUARTERS, 7)),
+            dma((QUARTERS, 8)),
+            dma((QUARTERS, 8)),
+            dma((QUARTERS,)),
             dma((QUARTERS, 4)),
-            dma((QUARTERS, 4)),
-            dma((QUARTERS, N_COL - 1)),
-            dma((QUARTERS, N_COL - 1)),
-            dma((QUARTERS, N_COL - 1)),
-            dma((QUARTERS, N_COL - 1)),
-            dma((10,)),
-            dma((10,)),
+            dma((QUARTERS, 2)),
+            dma((QUARTERS, 2)),
+            dma((QUARTERS,)),
+            dma((QUARTERS,)),
+            dma((QUARTERS,)),
+            dma((QUARTERS,)),
+            dma((4,)),
+            dma((4,)),
         ],
         compiler_params=pltpu.CompilerParams(
             collective_id=0, has_side_effects=True, vmem_limit_bytes=VMEM_BYTES
@@ -691,13 +718,14 @@
         name="decode",
     )(
         tokens.T,
-        layer_norm_gain.reshape(1, feats),
+        layer_norm_gain,
         query_weight,
         kv_weight,
         output_weight_matrix,
         kv_cache,
         lengths,
     )
+    branch, new_kv = hand_over(branch, new_kv)
     return branch.T, new_kv
 
 

time: 106 us -> 92.4 us (0.87)
  Pallas kernels: 98.8 us -> 90 us
  local copies, waits for them, and re-layouts: 4.21 us -> 0 us
    pallas_call x1, Pallas kernels: 98.8 us -> 88.3 us  [shards(): pl.pallas_call(functools.partial(kernel, feats * devices), out_shape=(jax...]
    unnamed x2 -> x0, local copies, waits for them, and re-layouts: 2.99 us -> none
    pallas_call x0 -> x1, Pallas kernels: none -> 1.7 us  [hand_over(): pl.pallas_call(hand_over_kernel, out_shape=(jax.ShapeDtypeStruct(branch.s...]
    reshape x1 -> x0, local copies, waits for them, and re-layouts: 1.22 us -> none  [shards(): layer_norm_gain.reshape(1, feats)]
where the time goes in v3:
time: 92.4 us; the launch traced here: 90.6 us
  Pallas kernels  90 us (97%)
    pallas_call x1, Pallas kernels, shards(): pl.pallas_call(functools.partial(kernel, feats * devices), out_shape=(jax...  88.3 us

profile of v3, /device:TPU:8, one launch (start us, length us, event | category | flops | bytes accessed | tf_op | source)
XLA Modules:
  0.0 90.6 jit_solution(8981637084919195828)
XLA Ops:
  0.6 88.3 %decode.1 = (bf16[144,1024]{1,0:T(8,128)(2,1)}, bf16[8,512]{1,0:T(8,128)(2,1)}) custom-call(bf16[144,1024]{1,0:T(8,128)(2,1)} %bitcast.2, bf16[144]{0:T(256)(128)(2,1)} %gain.1, bf16[2304,768]{1,0:T(8,128)(2,1)} %wq.1, bf16[2304,512]{1,0:T(8,128)(2,1)} %wkv.1, bf16[768,2304]{1,0:T(8,128)(2,1)} %wo.1, bf16[8,2048,512]{2,1,0:T(8,128)(2,1)} %cache.1, s32[8]{0:T(128)} %lengths.1), custom_call_target="tpu_custom_call" | custom-call | tf_op jit(solution)/shard_map/decode/pallas_call | solution.py:656
  88.9 1.7 %hand_over.1 = (bf16[144,1024]{1,0:T(8,128)(2,1)}, bf16[8,512]{1,0:T(8,128)(2,1)}) custom-call(bf16[144,1024]{1,0:T(8,128)(2,1)} %get-tuple-element.6.branch, bf16[8,512]{1,0:T(8,128)(2,1)} %get-tuple-element.7.new_kv), custom_call_target="tpu_custom_call" | custom-call | tf_op jit(solution)/shard_map/hand_over/pallas_call | solution.py:629

commit v4 on v3

v4 whole, which is shorter than its diff:
```python
import functools

import jax
import jax.numpy as jnp
from jax import lax
from jax.experimental import pallas as pl
from jax.experimental.pallas import tpu as pltpu
from jax.sharding import PartitionSpec as P

MESH = pl.DeviceIdType.MESH
EPSILON = 1e-05
NEGATIVE_FLOOR = -1e30
HD = 256
SIDE = 4
N_COL = SIDE * SIDE
N_ROW = 8
ROWS_DEV = 8
LANES = 128
GROUPS = ROWS_DEV
CUT, REST = 80, 64
(
    ST_X,
    ST_Z,
    ST_Y,
    ST_C,
    ST_END,
    FIRST,
    FIRST_ON,
    SECOND,
    SECOND_ON,
    PROJECT,
    SUM_CORES,
    ROWS_OUT,
    ATTEND,
    CONTEXTS_OUT,
    CONTEXTS_ON,
    PROJECT_OUT,
    SUM_1B,
    SUM_2A,
    SUM_2B,
    SUM_END,
) = range(20)

ORDER = [
    (FIRST, 3), (FIRST, 7), (FIRST, 0), (ST_X, 0), (FIRST, 5), (FIRST, 1),
    (FIRST, 2), (FIRST, 6), (FIRST_ON, 3), (FIRST_ON, 7), (FIRST_ON, 0), (FIRST, 4),
    (ST_Z, 0), (FIRST_ON, 5), (FIRST_ON, 2), (FIRST_ON, 1), (FIRST_ON, 6), (SECOND, 3),
    (SECOND, 7), (SECOND, 0), (ST_Y, 0), (SECOND_ON, 3), (ST_C, 0), (SECOND, 2),
    (SECOND_ON, 7), (ST_END, 0), (SECOND_ON, 0), (SECOND, 5), (SECOND, 6), (PROJECT, 3),
    (SECOND_ON, 2), (FIRST_ON, 4), (SUM_CORES, 3), (PROJECT, 7), (PROJECT, 0), (SUM_CORES, 7),
    (SECOND_ON, 5), (SUM_CORES, 0), (SECOND, 1), (ROWS_OUT, 3), (SECOND_ON, 6), (PROJECT, 2),
    (SECOND, 4), (PROJECT, 5), (SUM_CORES, 2), (ROWS_OUT, 7), (SECOND_ON, 1), (SUM_CORES, 5),
    (ROWS_OUT, 0), (PROJECT, 6), (ATTEND, 3), (SECOND_ON, 4), (ROWS_OUT, 2), (PROJECT, 1),
    (SUM_CORES, 6), (ATTEND, 7), (ROWS_OUT, 5), (PROJECT, 4), (CONTEXTS_OUT, 3), (SUM_CORES, 1),
    (ATTEND, 0), (SUM_CORES, 4), (ATTEND, 2), (ROWS_OUT, 6), (CONTEXTS_OUT, 7), (ATTEND, 5),
    (CONTEXTS_ON, 3), (ROWS_OUT, 1), (CONTEXTS_OUT, 0), (PROJECT_OUT, 3), (ROWS_OUT, 4), (CONTEXTS_OUT, 2),
    (CONTEXTS_ON, 7), (ATTEND, 6), (PROJECT_OUT, 7), (CONTEXTS_OUT, 5), (CONTEXTS_ON, 0), (SUM_1B, 3),
    (ATTEND, 1), (PROJECT_OUT, 0), (ATTEND, 4), (SUM_1B, 7), (CONTEXTS_ON, 2), (CONTEXTS_OUT, 6),
    (CONTEXTS_ON, 5), (PROJECT_OUT, 2), (PROJECT_OUT, 5), (SUM_1B, 0), (CONTEXTS_OUT, 1), (CONTEXTS_OUT, 4),
    (SUM_2A, 3), (CONTEXTS_ON, 6), (SUM_1B, 2), (PROJECT_OUT, 6), (CONTEXTS_ON, 1), (SUM_1B, 5),
    (CONTEXTS_ON, 4), (PROJECT_OUT, 1), (PROJECT_OUT, 4), (SUM_2A, 7), (SUM_1B, 6), (SUM_1B, 1),
    (SUM_1B, 4), (SUM_2A, 6), (SUM_2A, 5), (SUM_2A, 2), (SUM_2B, 7), (SUM_2A, 0),
    (SUM_2A, 1), (SUM_2A, 4), (SUM_2B, 6), (SUM_2B, 2), (SUM_2B, 3), (SUM_2B, 1),
    (SUM_2B, 0), (SUM_2B, 5), (SUM_2B, 4), (SUM_END, 2), (SUM_END, 6), (SUM_END, 3),
    (SUM_END, 7), (SUM_END, 0), (SUM_END, 1), (SUM_END, 5), (SUM_END, 4),
]
VMEM_BYTES = 60 * 1024 * 1024
F32, BF16 = jnp.float32, jnp.bfloat16


def rcopy(src, dst, send_sem, recv_sem, device):
    return pltpu.make_async_remote_copy(
        src_ref=src,
        dst_ref=dst,
        send_sem=send_sem,
        recv_sem=recv_sem,
        device_id=device,
        device_id_type=MESH,
    )


def along(ax, x, z, step):
    if ax == 0:
        return lax.rem(x + step + SIDE, SIDE) * SIDE + z
    return x * SIDE + lax.rem(z + step + SIDE, SIDE)


def loop(low, high, body):
    def step(i, carry):
        body(i)
        return carry

    lax.fori_loop(low, high, step, 0)


OTHERS = sorted(
    [(i, k) for i in range(SIDE) for k in range(SIDE) if (i, k) != (0, 0)],
    key=lambda at: -min(at[0], SIDE - at[0]) - min(at[1], SIDE - at[1]),
)


def landed(ref, sem):
    pltpu.make_async_copy(ref, ref, sem).wait()


def greet(peers):
    barrier = pltpu.get_barrier_semaphore()
    for peer in peers:
        pl.semaphore_signal(barrier, inc=1, device_id=peer, device_id_type=MESH)


def feats_of(ax, v):
    return (0, CUT) if ax == v else (CUT, REST)


def part_of(ax, v, si):
    low, n = feats_of(ax, v)
    half = (n + 16) // 32 * 16
    return (low, half) if si == 0 else (low + half, n - half)


def by_parity(s, do):
    for v in (0, 1):
        pl.when(lax.rem(s, 2) == v)(lambda v=v: do(v))


def add_into(ref, *terms):
    total = ref[...].astype(F32)
    for term in terms:
        total = total + term[...].astype(F32)
    ref[...] = total.astype(BF16)


def kernel(
    n_features,
    tok,
    gain,
    wq,
    wkv,
    wo,
    cache,
    lengths,
    out,
    kv_out,
    perm,
    xbuf,
    qw,
    ow,
    kvc,
    gexp,
    xn,
    pq,
    pqr,
    yq,
    yqr,
    slab,
    slabr,
    cslab,
    cslabr,
    fold,
    cfold,
    qt,
    kvf,
    allctx,
    pbuf,
    r1a,
    r1b,
    r2a,
    r2b,
    ot,
    stx,
    stz,
    sty,
    stc,
    smsg,
    zmsg,
    ymsg,
    cmsg,
    mi,
    w_sem,
    k_sem,
    gs,
    gr,
    os_,
    or_,
    ps,
    pr,
    as_,
    ar,
    cs,
    cr,
    ss,
    sr,
):
    r, c = lax.axis_index("row"), lax.axis_index("col")
    x, z = lax.div(c, SIDE), lax.rem(c, SIDE)
    y, core = lax.div(r, 2), lax.rem(r, 2)
    partner = r + 1 - 2 * core
    feats = tok.shape[0]
    head_cols = wq.shape[1]
    q_parts = head_cols // LANES
    wide_parts = q_parts + 1
    wide = wide_parts * LANES

    def other(number):
        i, k = OTHERS[number]
        return lax.rem(x + i, SIDE) * SIDE + lax.rem(z + k, SIDE)

    def other_y(d):
        return lax.rem(r + 2 * d + 2, N_ROW)

    peers = [(r, other(d)) for d in range(N_COL - 1)]
    peers += [(other_y(d), c) for d in range(3)] + [(partner, c)]
    greet(peers)

    load_q = pltpu.make_async_copy(wq, qw.at[:, pl.ds(0, head_cols)], w_sem.at[0])
    load_kv = pltpu.make_async_copy(
        wkv.at[:, pl.ds(pl.multiple_of(x * LANES, LANES), LANES)],
        qw.at[:, pl.ds(head_cols, LANES)],
        w_sem.at[1],
    )
    load_o = pltpu.make_async_copy(wo, ow, w_sem.at[2])
    load_q.start()
    load_kv.start()

    def load_cache(b):
        return pltpu.make_async_copy(cache.at[b], kvc.at[b], k_sem.at[b])

    loop(0, ROWS_DEV, lambda b: load_cache(b).start())
    load_o.start()

    row = lax.broadcasted_iota(jnp.int32, (N_ROW * LANES, LANES), 0)
    lane = lax.broadcasted_iota(jnp.int32, (N_ROW * LANES, LANES), 1)
    same = lax.div(row, ROWS_DEV) == lane
    for s in range(GROUPS):
        hit = jnp.logical_and(same, lax.rem(row, ROWS_DEV) == s)
        perm[s] = jnp.where(hit, 1.0, 0.0).astype(BF16)

    sums, squares = [], []
    for s in range(GROUPS):
        t = jnp.dot(tok[...], perm[s], preferred_element_type=F32)
        xbuf[s, x, z] = t.astype(BF16)
        sums.append(jnp.sum(t, axis=0, keepdims=True))
        squares.append(jnp.sum(t * t, axis=0, keepdims=True))
    smsg[0:8] = jnp.concatenate(sums, axis=0)
    smsg[8:16] = jnp.concatenate(squares, axis=0)
    gains = gain[...].astype(F32).reshape(1, feats)
    smsg[16:24] = jnp.zeros((8, LANES), F32)
    smsg[16:17] = gains[:, 0:LANES]
    smsg[17:18, 0 : feats - LANES] = gains[:, LANES:feats]
    stx[x] = smsg[...]

    fold[...] = jnp.zeros_like(fold)
    cfold[...] = jnp.zeros_like(cfold)
    pl.semaphore_wait(pltpu.get_barrier_semaphore(), len(peers))

    def stat_x(d):
        return rcopy(smsg, stx.at[x], ss.at[0], sr.at[0], (r, along(0, x, z, d + 1)))

    def stat_z(d):
        return rcopy(zmsg, stz.at[z], ss.at[1], sr.at[1], (r, along(1, x, z, d + 1)))

    def stat_y(d):
        return rcopy(ymsg, sty.at[y], ss.at[2], sr.at[2], (other_y(d), c))

    stat_c = rcopy(cmsg, stc.at[core], ss.at[3], sr.at[3], (partner, c))

    def mid(ax):
        return x if ax == 0 else z

    def end(ax):
        return z if ax == 0 else x

    def blocks(buf, ax, s, i, low, n, feats):
        i = lax.rem(i + SIDE, SIDE)
        some, f = pl.ds(low, n), pl.ds(*feats)
        return buf.at[s, some, i, f] if ax == 0 else buf.at[s, i, some, f]

    def block(buf, ax, s, i, feats):
        i = lax.rem(i + SIDE, SIDE)
        f = pl.ds(*feats)
        return buf.at[s, i, z, f] if ax == 0 else buf.at[s, x, i, f]

    def first(ax, s, si, v):
        here = block(xbuf, ax, s, mid(ax), feats_of(ax, v))
        return rcopy(here, here, gs.at[0], gr.at[s, 0], (r, along(ax, x, z, 1 - 2 * si)))

    def first_on(ax, s, si, v):
        way = 1 - 2 * si
        ref = block(xbuf, ax, s, mid(ax) - way, part_of(ax, v, si))
        return rcopy(ref, ref, gs.at[1], gr.at[s, 1], (r, along(ax, x, z, way)))

    def second(ax, s, si, v):
        ref = blocks(xbuf, ax, s, end(ax), 0, SIDE, feats_of(ax, v))
        return rcopy(ref, ref, gs.at[2], gr.at[s, 2], (r, along(1 - ax, x, z, 1 - 2 * si)))

    def second_on(ax, s, si, v):
        way = 1 - 2 * si
        ref = blocks(xbuf, ax, s, end(ax) - way, 2 * si, 2, feats_of(ax, v))
        return rcopy(ref, ref, gs.at[3], gr.at[s, 3], (r, along(1 - ax, x, z, way)))

    def ways(s, send):
        def do(v):
            for si in (0, 1):
                for ax in (0, 1):
                    send(ax, s, si, v).start()

        by_parity(s, do)

    def stats_x(s):
        for d in range(3):
            stat_x(d).start()

    def stats_z(s):
        landed(stx.at[pl.ds(0, 3)], sr.at[0])
        zmsg[0:16] = stx[0, 0:16] + stx[1, 0:16] + stx[2, 0:16] + stx[3, 0:16]
        for i in range(SIDE):
            zmsg[16 + 8 * i : 24 + 8 * i] = stx[i, 16:24]
        stz[z] = zmsg[...]
        for d in range(3):
            stat_z(d).start()

    def spread(i):
        rows = stz[i % SIDE, pl.ds(pl.multiple_of(16 + 8 * (i // SIDE), 8), 8)]
        gexp[i, 0:128] = jnp.broadcast_to(rows[0:1], (128, 128)).T
        gexp[i, 128:feats] = jnp.broadcast_to(rows[1:2], (128, 128)).T[0 : feats - 128]

    def stats_y(s):
        landed(stz.at[pl.ds(0, 3)], sr.at[1])
        ymsg[...] = stz[0, 0:16] + stz[1, 0:16] + stz[2, 0:16] + stz[3, 0:16]
        sty[y] = ymsg[...]
        for d in range(3):
            stat_y(d).start()
        loop(0, N_COL, spread)

    def stats_core(s):
        landed(sty.at[pl.ds(0, 3)], sr.at[2])
        cmsg[...] = sty[0] + sty[1] + sty[2] + sty[3]
        stc[core] = cmsg[...]
        stat_c.start()

    def stats_end(s):
        stat_c.wait_recv()
        total = stc[0] + stc[1]
        average = total[0:8] / n_features
        mi[0:8] = average
        mi[8:16] = lax.rsqrt(total[8:16] / n_features - average * average + EPSILON)
        load_q.wait()
        load_kv.wait()
        load_o.wait()

    def tokens_first(s):
        ways(s, first)

    def tokens_first_on(s):
        landed(xbuf.at[s, 0, pl.ds(0, 2)], gr.at[s, 0])
        ways(s, first_on)

    def tokens_second(s):
        landed(xbuf.at[s, 0, 0], gr.at[s, 1])
        ways(s, second)

    def tokens_second_on(s):
        landed(xbuf.at[s, pl.ds(0, 2)], gr.at[s, 2])
        ways(s, second_on)

    def to_partner(s):
        return rcopy(pq.at[s, 1 - core], pqr.at[s], ps.at[0], pr.at[s, 0], (partner, c))

    def project(s):
        landed(xbuf.at[s, 0], gr.at[s, 3])
        mean, inverse = mi[pl.ds(s, 1), :], mi[pl.ds(8 + s, 1), :]
        for i in range(N_COL):
            t = xbuf[s, i // SIDE, i % SIDE].astype(F32)
            xn[feats * i : feats * (i + 1)] = ((t - mean) * inverse * gexp[i]).astype(BF16)
        partial = lax.dot_general(
            xn[...], qw[...], (((0,), (0,)), ((), ())), preferred_element_type=F32
        ).astype(BF16)
        for i in range(N_ROW):
            pq[s, i % 2, i // 2] = partial[N_COL * i : N_COL * (i + 1)]
        to_partner(s).start()

    def to_y(s, d):
        to = other_y(d)
        return rcopy(
            yq.at[s, lax.div(to, 2)], yqr.at[s, y], ps.at[1], pr.at[s, 1], (to, c)
        )

    def sum_cores(s):
        to_partner(s).wait_recv()
        yq[s] = (pq[s, core].astype(F32) + pqr[s].astype(F32)).astype(BF16)
        for d in range(3):
            to_y(s, d).start()
        yqr[s, y] = yq[s, y]

    def scatter(src, dst, send_sem, recv_sem, s, d):
        to = other(d)
        return rcopy(src.at[s, to], dst.at[s, c], send_sem.at[0], recv_sem.at[s], (r, to))

    def rows_out(s):
        landed(yqr.at[s, pl.ds(0, 3)], pr.at[s, 1])
        total = yqr[s, 0].astype(F32)
        for i in range(1, SIDE):
            total = total + yqr[s, i].astype(F32)
        for k in range(wide_parts):
            fold[:, k, :] = total[:, LANES * k : LANES * (k + 1)]
        slab[s] = fold[...].astype(BF16)
        for d in range(N_COL - 1):
            scatter(slab, slabr, as_, ar, s, d).start()
        slabr[s, c] = slab[s, c]

    scale = HD**-0.5

    def attend(s):
        landed(slabr.at[s, pl.ds(0, N_COL - 1)], ar.at[s])
        fold[...] = slabr[s].astype(F32)
        for k in range(q_parts):
            at = slice(N_COL * (k // 2), N_COL * (k // 2 + 1))
            qt[at, LANES * (k % 2) : LANES * (k % 2 + 1)] = fold[:, k, :].astype(BF16)
        for i in range(SIDE):
            kvf[s, 0:1, LANES * i : LANES * (i + 1)] = fold[SIDE * i, q_parts : q_parts + 1, :]
        load_cache(s).wait()
        q = qt[...]
        new_key, new_value = kvf[s, 0:1, :HD], kvf[s, 0:1, HD:]
        position = lax.broadcasted_iota(jnp.int32, (1, kvc.shape[1]), 1)
        scores = (
            lax.dot_general(
                q, kvc[s, :, :HD], (((1,), (1,)), ((), ())), preferred_element_type=F32
            )
            * scale
        )
        scores = jnp.where(position < lengths[s], scores, NEGATIVE_FLOOR)
        new_score = jnp.sum(q.astype(F32) * new_key, axis=1, keepdims=True) * scale
        top = jnp.maximum(jnp.max(scores, axis=1, keepdims=True), new_score)
        weights = jnp.exp(scores - top)
        new_weight = jnp.exp(new_score - top)
        total = jnp.sum(weights, axis=1, keepdims=True) + new_weight
        context = jnp.dot(weights.astype(BF16), kvc[s, :, HD:], preferred_element_type=F32)
        context = context + new_weight.astype(BF16).astype(F32) * new_value
        context = context / total
        for k in range(q_parts):
            cfold[:, k, :] = context[
                N_COL * (k // 2) : N_COL * (k // 2 + 1), LANES * (k % 2) : LANES * (k % 2 + 1)
            ]
        cslab[s] = cfold[...].astype(BF16)
        for d in range(N_COL - 1):
            scatter(cslab, cslabr, cs, cr, s, d).start()
        cslabr[s, c] = cslab[s, c]

    def share(s, d):
        to = (other_y(d), c)
        ref = allctx.at[s, r]
        return rcopy(ref, ref, os_.at[0], or_.at[s, d], to)

    def pass_on(s, d):
        ref = allctx.at[s, lax.rem(r + 2 * (SIDE - 1 - d), N_ROW)]
        return rcopy(ref, ref, os_.at[0], or_.at[s, 3], (partner, c))

    def share_core(s):
        ref = allctx.at[s, r]
        return rcopy(ref, ref, os_.at[0], or_.at[s, 3], (partner, c))

    def contexts_out(s):
        landed(cslabr.at[s, pl.ds(0, N_COL - 1)], cr.at[s])
        cfold[...] = cslabr[s].astype(F32)
        for k in range(q_parts):
            allctx[s, r, :, LANES * k : LANES * (k + 1)] = cfold[:, k, :].astype(BF16)
        for d in range(3):
            share(s, d).start()
        share_core(s).start()

    def contexts_on(s):
        for d in range(3):
            share(s, d).wait_recv()
            pass_on(s, d).start()

    def group(ax, s, i, low, n, feats):
        i = lax.rem(i + SIDE, SIDE)
        some, f = pl.ds(low, n), pl.ds(*feats)
        return pbuf.at[s, i, some, f] if ax == 0 else pbuf.at[s, some, i, f]

    def single(ax, s, i, feats):
        i = lax.rem(i + SIDE, SIDE)
        f = pl.ds(*feats)
        return pbuf.at[s, x, i, f] if ax == 0 else pbuf.at[s, i, z, f]

    def send_1a(ax, s, si, v):
        f = feats_of(ax, v)
        src = group(ax, s, mid(ax) + 2, 2 * si, 2, f)
        to = (r, along(ax, x, z, 1 - 2 * si))
        return rcopy(src, r1a.at[s, si, :, pl.ds(*f)], gs.at[4], gr.at[s, 4], to)

    def send_1b(ax, s, si, v):
        f = feats_of(ax, v)
        src = group(ax, s, mid(ax) + 1 - 2 * si, 0, SIDE, f)
        to = (r, along(ax, x, z, 1 - 2 * si))
        return rcopy(src, r1b.at[s, si, :, pl.ds(*f)], gs.at[5], gr.at[s, 5], to)

    def send_2a(ax, s, si, v):
        f = part_of(ax, v, si)
        src = single(ax, s, end(ax) + 2, f)
        to = (r, along(1 - ax, x, z, 1 - 2 * si))
        return rcopy(src, r2a.at[s, pl.ds(*f)], gs.at[6], gr.at[s, 6], to)

    def send_2b(ax, s, si, v):
        f = feats_of(ax, v)
        src = single(ax, s, end(ax) + 1 - 2 * si, f)
        to = (r, along(1 - ax, x, z, 1 - 2 * si))
        return rcopy(src, r2b.at[s, si, pl.ds(*f)], gs.at[7], gr.at[s, 7], to)

    def project_out(s):
        landed(allctx.at[s, pl.ds(0, 4)], or_.at[s, 3])
        context = allctx[s].reshape(LANES, head_cols)
        term = jnp.dot(context, ow[...], preferred_element_type=F32)
        turned = term.astype(BF16).T
        for i in range(N_COL):
            pbuf[s, i // SIDE, i % SIDE] = turned[feats * i : feats * (i + 1)]
        ways(s, send_1a)

    def sum_1b(s):
        landed(pbuf.at[s, 0], gr.at[s, 4])

        def do(v):
            for ax in (0, 1):
                f = feats_of(ax, v)
                for si in (0, 1):
                    add_into(
                        group(ax, s, mid(ax) + 1 - 2 * si, 2 * si, 2, f),
                        r1a.at[s, si, :, pl.ds(*f)],
                    )
                    send_1b(ax, s, si, v).start()

        by_parity(s, do)

    def sum_2a(s):
        landed(pbuf.at[s, pl.ds(0, 2)], gr.at[s, 5])

        def do(v):
            for ax in (0, 1):
                f = feats_of(ax, v)
                add_into(
                    group(ax, s, mid(ax), 0, SIDE, f),
                    r1b.at[s, 0, :, pl.ds(*f)],
                    r1b.at[s, 1, :, pl.ds(*f)],
                )
                for si in (0, 1):
                    send_2a(ax, s, si, v).start()

        by_parity(s, do)

    def sum_2b(s):
        landed(pbuf.at[s, 0, 0], gr.at[s, 6])

        def do(v):
            for ax in (0, 1):
                for si in (0, 1):
                    f = part_of(ax, v, si)
                    add_into(single(ax, s, end(ax) + 1 - 2 * si, f), r2a.at[s, pl.ds(*f)])
                    send_2b(ax, s, si, v).start()

        by_parity(s, do)

    def sum_end(s):
        landed(pbuf.at[s, 0, pl.ds(0, 2)], gr.at[s, 7])
        total = pbuf[s, x, z].astype(F32) + r2b[s, 0].astype(F32) + r2b[s, 1].astype(F32)
        ot[s] = total.astype(BF16)

    steps = {
        ST_X: stats_x,
        ST_Z: stats_z,
        ST_Y: stats_y,
        ST_C: stats_core,
        ST_END: stats_end,
        FIRST: tokens_first,
        FIRST_ON: tokens_first_on,
        SECOND: tokens_second,
        SECOND_ON: tokens_second_on,
        PROJECT: project,
        SUM_CORES: sum_cores,
        ROWS_OUT: rows_out,
        ATTEND: attend,
        CONTEXTS_OUT: contexts_out,
        CONTEXTS_ON: contexts_on,
        PROJECT_OUT: project_out,
        SUM_1B: sum_1b,
        SUM_2A: sum_2a,
        SUM_2B: sum_2b,
        SUM_END: sum_end,
    }

    def take(step, s, low, high):
        if high - low == 1:
            steps[low](s)
            return
        middle = (low + high) // 2
        pl.when(step < middle)(lambda: take(step, s, low, middle))
        pl.when(step >= middle)(lambda: take(step, s, middle, high))

    base = 256
    codes = [step * GROUPS + s for step, s in ORDER]
    codes += [0] * (-len(codes) % 3)

    def in_order(t):
        at, which = lax.div(t, 3), lax.rem(t, 3)
        word = jnp.int32(0)
        for i in range(0, len(codes), 3):
            number = codes[i] + base * (codes[i + 1] + base * codes[i + 2])
            word = jnp.where(at == i // 3, number, word)
        rest = lax.div(word, base)
        code = jnp.where(which == 0, word, jnp.where(which == 1, rest, lax.div(rest, base)))
        code = lax.rem(code, base)
        take(lax.div(code, GROUPS), lax.rem(code, GROUPS), 0, len(steps))

    loop(0, len(ORDER), in_order)

    total = jnp.zeros(out.shape, F32)
    for s in range(GROUPS):
        total = total + lax.dot_general(
            ot[s], perm[s], (((1,), (1,)), ((), ())), preferred_element_type=F32
        )
    out[...] = total.astype(BF16)
    fresh = [kvf[n, 0:1, :] for n in range(ROWS_DEV)]
    kv_out[...] = jnp.concatenate(fresh, axis=0).astype(BF16)

    landed(stx.at[pl.ds(0, 3)], ss.at[0])
    landed(stz.at[pl.ds(0, 3)], ss.at[1])
    landed(sty.at[pl.ds(0, 3)], ss.at[2])
    stat_c.wait_send()

    landed(xbuf.at[0], gs.at[0])
    landed(xbuf.at[0, pl.ds(0, 2)], gs.at[1])
    landed(xbuf.at[pl.ds(0, 4)], gs.at[2])
    landed(xbuf.at[pl.ds(0, 2)], gs.at[3])
    landed(pbuf.at[pl.ds(0, 2)], gs.at[4])
    landed(pbuf.at[pl.ds(0, 4)], gs.at[5])
    landed(pbuf.at[0, pl.ds(0, 2)], gs.at[6])
    landed(pbuf.at[0], gs.at[7])
    landed(pqr, ps.at[0])
    landed(yqr.at[:, pl.ds(0, 3)], ps.at[1])
    landed(slab.at[:, pl.ds(0, N_COL - 1)], as_.at[0])
    landed(cslab.at[:, pl.ds(0, N_COL - 1)], cs.at[0])
    landed(allctx.at[:, pl.ds(0, 7)], os_.at[0])


def hand_over_kernel(branch, new_kv, branch_out, new_kv_out):
    branch_out[...] = branch[...]
    new_kv_out[...] = new_kv[...]


def hand_over(branch, new_kv):
    vmem = pl.BlockSpec(memory_space=pltpu.VMEM)
    return pl.pallas_call(
        hand_over_kernel,
        out_shape=(
            jax.ShapeDtypeStruct(branch.shape, branch.dtype),
            jax.ShapeDtypeStruct(new_kv.shape, new_kv.dtype),
        ),
        in_specs=[vmem, vmem],
        out_specs=(vmem, vmem),
        name="hand_over",
    )(branch, new_kv)


def shards(
    tokens, layer_norm_gain, query_weight, kv_weight, output_weight_matrix, kv_cache, lengths
):
    devices = lax.axis_size("row") * lax.axis_size("col")
    rows, feats = tokens.shape
    depth, head_cols = query_weight.shape
    heads = head_cols * N_COL // HD
    kv_cols = kv_weight.shape[1]
    wide = head_cols + LANES
    vmem = pl.BlockSpec(memory_space=pltpu.VMEM)
    smem = pl.BlockSpec(memory_space=pltpu.SMEM)
    anywhere = pl.BlockSpec(memory_space=pl.ANY)
    dma = pltpu.SemaphoreType.DMA
    slabs = pltpu.VMEM((GROUPS, N_COL, 8, LANES), BF16)
    branch, new_kv = pl.pallas_call(
        functools.partial(kernel, feats * devices),
        out_shape=(
            jax.ShapeDtypeStruct((feats, rows), BF16),
            jax.ShapeDtypeStruct((ROWS_DEV, kv_cols), BF16),
        ),
        in_specs=[vmem, vmem, anywhere, anywhere, anywhere, anywhere, smem],
        out_specs=(vmem, vmem),
        scratch_shapes=[
            pltpu.VMEM((GROUPS, rows, LANES), BF16),
            pltpu.VMEM((GROUPS, SIDE, SIDE, feats, LANES), BF16),
            pltpu.VMEM((depth, wide), BF16),
            pltpu.VMEM(output_weight_matrix.shape, BF16),
            pltpu.VMEM(kv_cache.shape, BF16),
            pltpu.VMEM((N_COL, feats, LANES), F32),
            pltpu.VMEM((depth, LANES), BF16),
            pltpu.VMEM((GROUPS, 2, SIDE, N_COL, wide), BF16),
            pltpu.VMEM((GROUPS, SIDE, N_COL, wide), BF16),
            pltpu.VMEM((GROUPS, SIDE, N_COL, wide), BF16),
            pltpu.VMEM((GROUPS, SIDE, N_COL, wide), BF16),
            slabs,
            slabs,
            slabs,
            slabs,
            pltpu.VMEM((N_COL, 8, LANES), F32),
            pltpu.VMEM((N_COL, 8, LANES), F32),
            pltpu.VMEM((heads, HD), BF16),
            pltpu.VMEM((ROWS_DEV, 8, kv_cols), F32),
            pltpu.VMEM((GROUPS, N_ROW, N_COL, head_cols), BF16),
            pltpu.VMEM((GROUPS, SIDE, SIDE, feats, LANES), BF16),
            pltpu.VMEM((GROUPS, 2, 2, feats, LANES), BF16),
            pltpu.VMEM((GROUPS, 2, SIDE, feats, LANES), BF16),
            pltpu.VMEM((GROUPS, feats, LANES), BF16),
            pltpu.VMEM((GROUPS, 2, feats, LANES), BF16),
            pltpu.VMEM((GROUPS, feats, LANES), BF16),
            pltpu.VMEM((SIDE, 24, LANES), F32),
            pltpu.VMEM((SIDE, 48, LANES), F32),
            pltpu.VMEM((SIDE, 16, LANES), F32),
            pltpu.VMEM((2, 16, LANES), F32),
            pltpu.VMEM((24, LANES), F32),
            pltpu.VMEM((48, LANES), F32),
            pltpu.VMEM((16, LANES), F32),
            pltpu.VMEM((16, LANES), F32),
            pltpu.VMEM((16, LANES), F32),
            dma((3,)),
            dma((ROWS_DEV,)),
            dma((8,)),
            dma((GROUPS, 8)),
            dma((1,)),
            dma((GROUPS, 4)),
            dma((2,)),
            dma((GROUPS, 2)),
            dma((1,)),
            dma((GROUPS,)),
            dma((1,)),
            dma((GROUPS,)),
            dma((4,)),
            dma((4,)),
        ],
        compiler_params=pltpu.CompilerParams(
            collective_id=0, has_side_effects=True, vmem_limit_bytes=VMEM_BYTES
        ),
        name="decode",
    )(
        tokens.T,
        layer_norm_gain,
        query_weight,
        kv_weight,
        output_weight_matrix,
        kv_cache,
        lengths,
    )
    branch, new_kv = hand_over(branch, new_kv)
    return branch.T, new_kv


def solution(mesh):
    placed = (
        P(None, ("row", "col")),
        P(("row", "col")),
        P("row", "col"),
        P("row", None),
        P("col", "row"),
        P(("row", "col"), None, None),
        P(("row", "col")),
    )
    return jax.shard_map(
        shards,
        mesh=mesh,
        in_specs=placed,
        out_specs=(P(None, ("row", "col")), P(("row", "col"), None)),
        check_vma=False,
    )
```

time: 92.4 us -> 88.2 us (0.955)
  Pallas kernels: 90 us -> 86.4 us
    pallas_call x1, Pallas kernels: 88.3 us -> 84.7 us  [shards(): pl.pallas_call(functools.partial(kernel, feats * devices), out_shape=(jax...]
where the time goes in v4:
time: 88.2 us; the launch traced here: 87 us
  Pallas kernels  86.4 us (98%)
    pallas_call x1, Pallas kernels, shards(): pl.pallas_call(functools.partial(kernel, feats * devices), out_shape=(jax...  84.7 us

profile of v4, /device:TPU:8, one launch (start us, length us, event | category | flops | bytes accessed | tf_op | source)
XLA Modules:
  0.0 87.0 jit_solution(12853046448439587451)
XLA Ops:
  0.6 84.7 %decode.1 = (bf16[144,1024]{1,0:T(8,128)(2,1)}, bf16[8,512]{1,0:T(8,128)(2,1)}) custom-call(bf16[144,1024]{1,0:T(8,128)(2,1)} %bitcast.2, bf16[144]{0:T(256)(128)(2,1)} %gain.1, bf16[2304,768]{1,0:T(8,128)(2,1)} %wq.1, bf16[2304,512]{1,0:T(8,128)(2,1)} %wkv.1, bf16[768,2304]{1,0:T(8,128)(2,1)} %wo.1, bf16[8,2048,512]{2,1,0:T(8,128)(2,1)} %cache.1, s32[8]{0:T(128)} %lengths.1), custom_call_target="tpu_custom_call" | custom-call | tf_op jit(solution)/shard_map/decode/pallas_call | solution.py:678
  85.3 1.7 %hand_over.1 = (bf16[144,1024]{1,0:T(8,128)(2,1)}, bf16[8,512]{1,0:T(8,128)(2,1)}) custom-call(bf16[144,1024]{1,0:T(8,128)(2,1)} %get-tuple-element.6.branch, bf16[8,512]{1,0:T(8,128)(2,1)} %get-tuple-element.7.new_kv), custom_call_target="tpu_custom_call" | custom-call | tf_op jit(solution)/shard_map/hand_over/pallas_call | solution.py:652

commit v5 on v4

--- a/solution.py
+++ b/solution.py
@@ -42,27 +42,27 @@
 ) = range(20)
 
 ORDER = [
-    (FIRST, 3), (FIRST, 7), (FIRST, 0), (ST_X, 0), (FIRST, 5), (FIRST, 1),
-    (FIRST, 2), (FIRST, 6), (FIRST_ON, 3), (FIRST_ON, 7), (FIRST_ON, 0), (FIRST, 4),
-    (ST_Z, 0), (FIRST_ON, 5), (FIRST_ON, 2), (FIRST_ON, 1), (FIRST_ON, 6), (SECOND, 3),
-    (SECOND, 7), (SECOND, 0), (ST_Y, 0), (SECOND_ON, 3), (ST_C, 0), (SECOND, 2),
-    (SECOND_ON, 7), (ST_END, 0), (SECOND_ON, 0), (SECOND, 5), (SECOND, 6), (PROJECT, 3),
-    (SECOND_ON, 2), (FIRST_ON, 4), (SUM_CORES, 3), (PROJECT, 7), (PROJECT, 0), (SUM_CORES, 7),
-    (SECOND_ON, 5), (SUM_CORES, 0), (SECOND, 1), (ROWS_OUT, 3), (SECOND_ON, 6), (PROJECT, 2),
-    (SECOND, 4), (PROJECT, 5), (SUM_CORES, 2), (ROWS_OUT, 7), (SECOND_ON, 1), (SUM_CORES, 5),
-    (ROWS_OUT, 0), (PROJECT, 6), (ATTEND, 3), (SECOND_ON, 4), (ROWS_OUT, 2), (PROJECT, 1),
-    (SUM_CORES, 6), (ATTEND, 7), (ROWS_OUT, 5), (PROJECT, 4), (CONTEXTS_OUT, 3), (SUM_CORES, 1),
-    (ATTEND, 0), (SUM_CORES, 4), (ATTEND, 2), (ROWS_OUT, 6), (CONTEXTS_OUT, 7), (ATTEND, 5),
-    (CONTEXTS_ON, 3), (ROWS_OUT, 1), (CONTEXTS_OUT, 0), (PROJECT_OUT, 3), (ROWS_OUT, 4), (CONTEXTS_OUT, 2),
-    (CONTEXTS_ON, 7), (ATTEND, 6), (PROJECT_OUT, 7), (CONTEXTS_OUT, 5), (CONTEXTS_ON, 0), (SUM_1B, 3),
-    (ATTEND, 1), (PROJECT_OUT, 0), (ATTEND, 4), (SUM_1B, 7), (CONTEXTS_ON, 2), (CONTEXTS_OUT, 6),
-    (CONTEXTS_ON, 5), (PROJECT_OUT, 2), (PROJECT_OUT, 5), (SUM_1B, 0), (CONTEXTS_OUT, 1), (CONTEXTS_OUT, 4),
-    (SUM_2A, 3), (CONTEXTS_ON, 6), (SUM_1B, 2), (PROJECT_OUT, 6), (CONTEXTS_ON, 1), (SUM_1B, 5),
-    (CONTEXTS_ON, 4), (PROJECT_OUT, 1), (PROJECT_OUT, 4), (SUM_2A, 7), (SUM_1B, 6), (SUM_1B, 1),
-    (SUM_1B, 4), (SUM_2A, 6), (SUM_2A, 5), (SUM_2A, 2), (SUM_2B, 7), (SUM_2A, 0),
-    (SUM_2A, 1), (SUM_2A, 4), (SUM_2B, 6), (SUM_2B, 2), (SUM_2B, 3), (SUM_2B, 1),
-    (SUM_2B, 0), (SUM_2B, 5), (SUM_2B, 4), (SUM_END, 2), (SUM_END, 6), (SUM_END, 3),
-    (SUM_END, 7), (SUM_END, 0), (SUM_END, 1), (SUM_END, 5), (SUM_END, 4),
+    (FIRST, 1), (ST_X, 0), (FIRST, 5), (FIRST, 6), (FIRST, 2), (FIRST, 3),
+    (FIRST, 7), (FIRST, 4), (FIRST_ON, 1), (ST_Z, 0), (FIRST, 0), (FIRST_ON, 6),
+    (FIRST_ON, 2), (FIRST_ON, 3), (FIRST_ON, 7), (FIRST_ON, 5), (FIRST_ON, 4), (SECOND, 1),
+    (SECOND, 2), (SECOND, 3), (ST_Y, 0), (SECOND_ON, 1), (SECOND, 4), (ST_C, 0),
+    (SECOND_ON, 2), (ST_END, 0), (SECOND_ON, 3), (SECOND, 5), (PROJECT, 1), (SUM_CORES, 1),
+    (SECOND_ON, 4), (FIRST_ON, 0), (SECOND, 7), (PROJECT, 2), (PROJECT, 3), (SUM_CORES, 2),
+    (SECOND_ON, 5), (SECOND, 6), (SUM_CORES, 3), (PROJECT, 4), (ROWS_OUT, 1), (SUM_CORES, 4),
+    (SECOND_ON, 7), (SECOND, 0), (PROJECT, 5), (ROWS_OUT, 2), (SECOND_ON, 6), (ROWS_OUT, 3),
+    (SUM_CORES, 5), (PROJECT, 7), (ATTEND, 1), (ROWS_OUT, 4), (SECOND_ON, 0), (PROJECT, 6),
+    (SUM_CORES, 7), (ATTEND, 2), (SUM_CORES, 6), (ATTEND, 3), (CONTEXTS_OUT, 1), (ROWS_OUT, 5),
+    (PROJECT, 0), (ATTEND, 4), (SUM_CORES, 0), (ROWS_OUT, 7), (CONTEXTS_OUT, 2), (CONTEXTS_ON, 1),
+    (ROWS_OUT, 6), (CONTEXTS_OUT, 3), (PROJECT_OUT, 1), (ATTEND, 5), (ROWS_OUT, 0), (CONTEXTS_OUT, 4),
+    (ATTEND, 7), (SUM_1B, 1), (CONTEXTS_ON, 2), (CONTEXTS_ON, 3), (ATTEND, 6), (PROJECT_OUT, 3),
+    (CONTEXTS_OUT, 5), (PROJECT_OUT, 2), (CONTEXTS_ON, 4), (ATTEND, 0), (PROJECT_OUT, 4), (CONTEXTS_OUT, 7),
+    (SUM_1B, 3), (CONTEXTS_OUT, 6), (SUM_1B, 2), (CONTEXTS_ON, 5), (PROJECT_OUT, 5), (SUM_1B, 4),
+    (CONTEXTS_OUT, 0), (CONTEXTS_ON, 7), (CONTEXTS_ON, 6), (PROJECT_OUT, 7), (PROJECT_OUT, 6), (SUM_1B, 5),
+    (CONTEXTS_ON, 0), (PROJECT_OUT, 0), (SUM_2A, 4), (SUM_1B, 7), (SUM_1B, 6), (SUM_1B, 0),
+    (SUM_2A, 7), (SUM_2A, 5), (SUM_2B, 4), (SUM_2A, 1), (SUM_2A, 2), (SUM_2A, 6),
+    (SUM_2A, 3), (SUM_2A, 0), (SUM_2B, 7), (SUM_2B, 5), (SUM_2B, 1), (SUM_2B, 6),
+    (SUM_2B, 3), (SUM_2B, 2), (SUM_2B, 0), (SUM_END, 5), (SUM_END, 3), (SUM_END, 7),
+    (SUM_END, 1), (SUM_END, 6), (SUM_END, 4), (SUM_END, 2), (SUM_END, 0),
 ]
 VMEM_BYTES = 60 * 1024 * 1024
 F32, BF16 = jnp.float32, jnp.bfloat16

time: 88.2 us -> 87.9 us (level)
  no operation moved by 1% of the time
where the time goes in v5:
time: 87.9 us; the launch traced here: 86.4 us
  Pallas kernels  85.8 us (98%)
    pallas_call x1, Pallas kernels, shards(): pl.pallas_call(functools.partial(kernel, feats * devices), out_shape=(jax...  84.1 us

profile of v5, /device:TPU:8, one launch (start us, length us, event | category | flops | bytes accessed | tf_op | source)
XLA Modules:
  0.0 86.4 jit_solution(16273371030730669068)
XLA Ops:
  0.6 84.1 %decode.1 = (bf16[144,1024]{1,0:T(8,128)(2,1)}, bf16[8,512]{1,0:T(8,128)(2,1)}) custom-call(bf16[144,1024]{1,0:T(8,128)(2,1)} %bitcast.2, bf16[144]{0:T(256)(128)(2,1)} %gain.1, bf16[2304,768]{1,0:T(8,128)(2,1)} %wq.1, bf16[2304,512]{1,0:T(8,128)(2,1)} %wkv.1, bf16[768,2304]{1,0:T(8,128)(2,1)} %wo.1, bf16[8,2048,512]{2,1,0:T(8,128)(2,1)} %cache.1, s32[8]{0:T(128)} %lengths.1), custom_call_target="tpu_custom_call" | custom-call | tf_op jit(solution)/shard_map/decode/pallas_call | solution.py:678
  84.7 1.7 %hand_over.1 = (bf16[144,1024]{1,0:T(8,128)(2,1)}, bf16[8,512]{1,0:T(8,128)(2,1)}) custom-call(bf16[144,1024]{1,0:T(8,128)(2,1)} %get-tuple-element.6.branch, bf16[8,512]{1,0:T(8,128)(2,1)} %get-tuple-element.7.new_kv), custom_call_target="tpu_custom_call" | custom-call | tf_op jit(solution)/shard_map/hand_over/pallas_call | solution.py:652
